TPU v7x, 256 devices: a whole 4x4x8 slice. The times are simulated.
256 devices in a mesh: dp: 8 (over y, core), expert: 32 (over x, z).
Axes of the slice: x: 4, y: 4, z: 8, core: 2. Of those that a mesh axis runs over, the one named last changes fastest.
Arguments:
- tokens: bfloat16 [32768, 2048], P(('dp', 'expert')), may hold values from -6 to 6
- cotangent: bfloat16 [32768, 2048], P(('dp', 'expert')), may hold values from -6 to 6
- routed_slots: int32 [32768, 2], P(('dp', 'expert')), may hold values from 0 to 31, all different within a row; in each aligned block of 128 rows (0 to 127, 128 to 255, ...) at most 10 rows name the same one
- route_probs: bfloat16 [32768, 2], P(('dp', 'expert')), may hold values from 0.049804688 to 1
- placement: int32 [32], replicated, may hold values from 0 to 15, as said below
- w_gate: bfloat16 [16, 768, 2048], P(None, 'expert'), may hold values from -0.125 to 0.125
- w_up: bfloat16 [16, 768, 2048], P(None, 'expert'), may hold values from -0.125 to 0.125
- w_down: bfloat16 [16, 768, 2048], P(None, 'expert'), may hold values from -0.21875 to 0.21875
Outputs:
- token_grad: bfloat16 [32768, 2048], P(('dp', 'expert'))
- prob_grad: bfloat16 [32768, 2], P(('dp', 'expert'))
- grad_gate: bfloat16 [16, 768, 2048], P(None, 'expert', 'dp')
- grad_up: bfloat16 [16, 768, 2048], P(None, 'expert', 'dp')
- grad_down: bfloat16 [16, 768, 2048], P(None, 'expert', 'dp')
Inputs may be any that keep to these rules, and one draw needn't show every extreme that they name: `routed_slots`: each token names 2 different slots. Of the 128 rows of one device, at most 10 name any one slot. `placement`: every expert is hosted by one slot or more.
All inputs are finite; a program needn't handle non-finite values.
Results may differ from a plain program's by a relative error of at most 0.018.
Values may be sent and summed in bfloat16 or wider, within the bound.
No kernel may reach another device: no remote copies, remote signals or barrier semaphores. Data moves between devices by JAX's collectives and lax.ppermute only.
A program may use at most 128 MiB of HBM per device.

v0:
```python
import jax
import jax.numpy as jnp
from jax import lax
from jax.sharding import PartitionSpec as P


def expert_rows(in_rows, cot_rows, prob_rows, gate_slab, up_slab, down_slab):
    gate_pre = jnp.dot(in_rows, gate_slab.T, preferred_element_type=jnp.float32)
    up_pre = jnp.dot(in_rows, up_slab.T, preferred_element_type=jnp.float32)
    sigma = jax.nn.sigmoid(gate_pre)
    swish = gate_pre * sigma
    hidden = (swish * up_pre).astype(jnp.bfloat16)
    out_rows = jnp.dot(hidden, down_slab, preferred_element_type=jnp.float32)
    prob_grad = jnp.sum(out_rows * cot_rows.astype(jnp.float32), axis=1).astype(jnp.bfloat16)
    scaled = (prob_rows.astype(jnp.float32)[:, None] * cot_rows.astype(jnp.float32)).astype(
        jnp.bfloat16
    )
    hidden_grad = jnp.dot(scaled, down_slab.T, preferred_element_type=jnp.float32)
    gate_grad = (hidden_grad * up_pre * sigma * (1.0 + gate_pre * (1.0 - sigma))).astype(
        jnp.bfloat16
    )
    up_grad = (hidden_grad * swish).astype(jnp.bfloat16)
    pair_grad = (
        jnp.dot(gate_grad, gate_slab, preferred_element_type=jnp.float32)
        + jnp.dot(up_grad, up_slab, preferred_element_type=jnp.float32)
    ).astype(jnp.bfloat16)
    part_gate = jnp.dot(gate_grad.T, in_rows, preferred_element_type=jnp.float32).astype(
        jnp.bfloat16
    )
    part_up = jnp.dot(up_grad.T, in_rows, preferred_element_type=jnp.float32).astype(jnp.bfloat16)
    part_down = jnp.dot(hidden.T, scaled, preferred_element_type=jnp.float32).astype(jnp.bfloat16)
    return (pair_grad, prob_grad, part_gate, part_up, part_down)


def on_device(tokens, cotangent, routed_slots, route_probs, placement, w_gate, w_up, w_down):
    slot_count = lax.axis_size("expert")
    tok_rows, model_width = tokens.shape
    choices = routed_slots.shape[1]
    capacity = max(2, (5 * tok_rows * choices + 4 * slot_count - 1) // (4 * slot_count))
    pair_count = tok_rows * choices
    expert_count, hidden_share, _ = w_gate.shape
    flat_slots = routed_slots.reshape(pair_count)
    one_hot = (flat_slots[:, None] == jnp.arange(slot_count, dtype=jnp.int32)[None, :]).astype(
        jnp.int32
    )
    before = jnp.cumsum(one_hot, axis=0) - one_hot
    bucket_rank = jnp.sum(before * one_hot, axis=1)
    bucket_cell = flat_slots * capacity + bucket_rank
    source_pair = jnp.full((slot_count * capacity,), pair_count, jnp.int32)
    source_pair = source_pair.at[bucket_cell].set(jnp.arange(pair_count, dtype=jnp.int32))
    filled = source_pair < pair_count
    safe_pair = jnp.minimum(source_pair, pair_count - 1)
    row_index = safe_pair // choices
    zero = jnp.zeros((), jnp.bfloat16)
    send_tokens = jnp.where(filled[:, None], tokens[row_index], zero).reshape(
        slot_count, capacity, model_width
    )
    send_cot = jnp.where(filled[:, None], cotangent[row_index], zero).reshape(
        slot_count, capacity, model_width
    )
    send_probs = jnp.where(filled, route_probs.reshape(pair_count)[safe_pair], zero).reshape(
        slot_count, capacity
    )
    wanted_gate = jnp.take(w_gate, placement, axis=0)
    wanted_up = jnp.take(w_up, placement, axis=0)
    wanted_down = jnp.take(w_down, placement, axis=0)
    gate_slab, up_slab, down_slab = (
        lax.all_to_all(wanted_gate, "expert", split_axis=0, concat_axis=1, tiled=True),
        lax.all_to_all(wanted_up, "expert", split_axis=0, concat_axis=1, tiled=True),
        lax.all_to_all(wanted_down, "expert", split_axis=0, concat_axis=1, tiled=True),
    )
    got_tokens, got_cot, got_probs = (
        lax.all_to_all(send_tokens, "expert", split_axis=0, concat_axis=0, tiled=True),
        lax.all_to_all(send_cot, "expert", split_axis=0, concat_axis=0, tiled=True),
        lax.all_to_all(send_probs, "expert", split_axis=0, concat_axis=0, tiled=True),
    )
    buffer_rows = slot_count * capacity
    pair_grad, prob_grad, part_gate, part_up, part_down = expert_rows(
        got_tokens.reshape(buffer_rows, model_width),
        got_cot.reshape(buffer_rows, model_width),
        got_probs.reshape(buffer_rows),
        gate_slab[0],
        up_slab[0],
        down_slab[0],
    )
    back_grad, back_prob = (
        lax.all_to_all(
            pair_grad.reshape(slot_count, capacity, model_width),
            "expert",
            split_axis=0,
            concat_axis=0,
            tiled=True,
        ),
        lax.all_to_all(
            prob_grad.reshape(slot_count, capacity),
            "expert",
            split_axis=0,
            concat_axis=0,
            tiled=True,
        ),
    )
    my_rows = back_grad.reshape(buffer_rows, model_width)[bucket_cell]
    token_grad = jnp.sum(
        my_rows.reshape(tok_rows, choices, model_width).astype(jnp.float32), axis=1
    ).astype(jnp.bfloat16)
    prob_out = back_prob.reshape(buffer_rows)[bucket_cell].reshape(tok_rows, choices)
    partials = jnp.stack([part_gate, part_up, part_down])
    hosted = placement[None, :] == jnp.arange(expert_count, dtype=jnp.int32)[:, None]
    slot_parts = partials.reshape(3, slot_count, hidden_share, model_width)
    home_parts = lax.all_to_all(slot_parts, "expert", split_axis=1, concat_axis=1, tiled=True)
    folded = jnp.einsum(
        "es,gsfd->gefd", hosted.astype(jnp.bfloat16), home_parts, preferred_element_type=jnp.float32
    )
    summed = lax.psum_scatter(folded.astype(jnp.bfloat16), "dp", scatter_dimension=3, tiled=True)
    return (token_grad, prob_out, summed[0], summed[1], summed[2])


def solution(mesh):
    placed = (
        P(("dp", "expert"), None),
        P(("dp", "expert"), None),
        P(("dp", "expert"), None),
        P(("dp", "expert"), None),
        P(),
        P(None, "expert", None),
        P(None, "expert", None),
        P(None, "expert", None),
    )
    return jax.shard_map(
        on_device,
        mesh=mesh,
        in_specs=placed,
        out_specs=(
            P(("dp", "expert"), None),
            P(("dp", "expert"), None),
            P(None, "expert", "dp"),
            P(None, "expert", "dp"),
            P(None, "expert", "dp"),
        ),
        check_vma=False,
    )
```

profile of v0, /device:TPU:9, one launch (start us, length us, event | category | flops | bytes accessed | tf_op | source)
XLA Modules:
  0.0 730.9 jit_solution(8581217829929897190)
XLA Ops:
  15.8 11.0 %all-to-all-start = ((bf16[32,1,10]{2,1,0:T(2,128)(2,1)}), bf16[32,1,10]{2,1,0:T(2,128)(2,1)S(1)}, u32[]{:S(2)}, u32[]{:S(2)}) async-start(bf16[32,1,10]{2,1,0:T(2,128)(2,1)} %all_to_all.53), calls=%async_computation | async-start | bytes 32768 | tf_op jit(solution)/shard_map/all_to_all | solution.py:75
  27.0 2.4 gather_fusion.2
  35.0 4.5 broadcast_select_fusion.4
  39.6 56.5 %all_to_all.63 = bf16[32,10,2048]{2,1,0:T(8,128)(2,1)} all-to-all(bf16[32,10,2048]{2,1,0:T(8,128)(2,1)} %get-tuple-element.29), channel_id=1, replica_groups=mesh['dp'=8,'expert'=32] {'expert'}, dimensions={0} | all-to-all | bytes 2621440 | tf_op jit(solution)/shard_map/all_to_all | solution.py:74
  96.0 8.8 %all-to-all-start.3 = ((bf16[32,10,2048]{2,1,0:T(8,128)(2,1)}), bf16[32,10,2048]{2,1,0:T(8,128)(2,1)}, u32[]{:S(2)}, u32[]{:S(2)}) async-start(bf16[32,10,2048]{2,1,0:T(8,128)(2,1)} %get-tuple-element.30), calls=%async_computation.3 | async-start | bytes 4194304 | tf_op jit(solution)/shard_map/all_to_all | solution.py:73
  107.3 2.4 gather_fusion.6
  112.2 6.7 broadcast_select_fusion.1
  118.9 34.6 %all-to-all-done.3 = bf16[32,10,2048]{2,1,0:T(8,128)(2,1)} async-done(((bf16[32,10,2048]{2,1,0:T(8,128)(2,1)}), bf16[32,10,2048]{2,1,0:T(8,128)(2,1)}, u32[]{:S(2)}, u32[]{:S(2)}) %all-to-all-start.3) | async-done | bytes 1310752 | tf_op jit(solution)/shard_map/all_to_all | solution.py:73
  153.5 77.1 %all_to_all.64 = bf16[32,24,2048]{2,1,0:T(8,128)(2,1)} all-to-all(bf16[32,24,2048]{2,1,0:T(8,128)(2,1)} %get-tuple-element.34), channel_id=1, replica_groups=mesh['dp'=8,'expert'=32] {'expert'}, dimensions={0} | all-to-all | bytes 6291456 | tf_op jit(solution)/shard_map/all_to_all | solution.py:68
  230.6 78.0 %all_to_all.65 = bf16[32,24,2048]{2,1,0:T(8,128)(2,1)} all-to-all(bf16[32,24,2048]{2,1,0:T(8,128)(2,1)S(1)} %copy-done.5), channel_id=1, replica_groups=mesh['dp'=8,'expert'=32] {'expert'}, dimensions={0} | all-to-all | bytes 6291456 | tf_op jit(solution)/shard_map/all_to_all | solution.py:70
  308.7 8.6 %all-to-all-start.4 = ((bf16[32,24,2048]{2,1,0:T(8,128)(2,1)}), bf16[32,24,2048]{2,1,0:T(8,128)(2,1)}, u32[]{:S(2)}, u32[]{:S(2)}) async-start(bf16[32,24,2048]{2,1,0:T(8,128)(2,1)} %get-tuple-element.33), calls=%async_computation.4 | async-start | bytes 6291456 | tf_op jit(solution)/shard_map/all_to_all | solution.py:69
  317.6 3.3 multiply_convert_fusion
  321.0 2.5 convert_element_type.91
  323.5 3.7 reshape.166
  327.2 2.5 reshape.159
  329.7 4.3 fusion.19
  336.2 54.3 %all-to-all-done.4 = bf16[32,24,2048]{2,1,0:T(8,128)(2,1)} async-done(((bf16[32,24,2048]{2,1,0:T(8,128)(2,1)}), bf16[32,24,2048]{2,1,0:T(8,128)(2,1)}, u32[]{:S(2)}, u32[]{:S(2)}) %all-to-all-start.4) | async-done | bytes 3145760 | tf_op jit(solution)/shard_map/all_to_all | solution.py:69
  390.5 3.9 multiply_convert_fusion.3
  394.4 3.6 convolution_convert_fusion.2
  398.0 3.5 convolution_convert_fusion.1
  401.5 3.6 convolution_convert_fusion
  405.1 8.4 %pad_maximum_fusion = bf16[3,32,24,2048]{3,2,0,1:T(8,128)(2,1)} fusion(bf16[1,32,24,2048]{3,2,0,1:T(8,128)(2,1)} %bitcast.69, bf16[1,32,24,2048]{3,2,0,1:T(8,128)(2,1)} %bitcast.68, bf16[1,32,24,2048]{3,2,0,1:T(8,128)(2,1)} %bitcast.67), kind=kLoop, calls=%fused_computation.9 | loop fusion | flops 9437184 | bytes 18874368 | tf_op jit(solution)/shard_map/stack | solution.py:107
  413.4 210.0 %all_to_all.66 = bf16[3,32,24,2048]{3,2,0,1:T(8,128)(2,1)S(1)} all-to-all(bf16[3,32,24,2048]{3,2,0,1:T(8,128)(2,1)} %pad_maximum_fusion), channel_id=1, replica_groups=mesh['dp'=8,'expert'=32] {'expert'}, dimensions={1} | all-to-all | bytes 18874368 | tf_op jit(solution)/shard_map/all_to_all | solution.py:110
  623.4 6.9 convert_bitcast_fusion
  630.4 4.0 fusion.5
  635.2 8.5 %all-to-all-start.7 = ((bf16[32,1,10]{2,1,0:T(2,128)(2,1)}), bf16[32,1,10]{2,1,0:T(2,128)(2,1)S(1)}, u32[]{:S(2)}, u32[]{:S(2)}) async-start(bf16[32,1,10]{2,1,0:T(2,128)(2,1)} %convert_element_type.111), calls=%async_computation.7 | async-start | bytes 32768 | tf_op jit(solution)/shard_map/all_to_all | solution.py:94
  643.7 3.1 fusion.21
  646.8 3.2 fusion.4
  652.2 9.1 %all-to-all-start.6 = ((bf16[32,10,2048]{2,1,0:T(8,128)(2,1)}), bf16[32,10,2048]{2,1,0:T(8,128)(2,1)}, u32[]{:S(2)}, u32[]{:S(2)}) async-start(bf16[32,10,2048]{2,1,0:T(8,128)(2,1)} %reshape.160), calls=%async_computation.6 | async-start | bytes 4194304 | tf_op jit(solution)/shard_map/all_to_all | solution.py:87
  664.2 46.2 %all-to-all-done.6 = bf16[32,10,2048]{2,1,0:T(8,128)(2,1)} async-done(((bf16[32,10,2048]{2,1,0:T(8,128)(2,1)}), bf16[32,10,2048]{2,1,0:T(8,128)(2,1)}, u32[]{:S(2)}, u32[]{:S(2)}) %all-to-all-start.6) | async-done | bytes 1310752 | tf_op jit(solution)/shard_map/all_to_all | solution.py:87
  710.4 2.5 reshape.161
  717.0 3.6 reduce_sum.34
  (74 shorter events, 35.1 us)
Async XLA Ops:
  7.2 97.7 %copy-start = (bf16[16,24,2048]{2,1,0:T(8,128)(2,1)S(1)}, bf16[16,24,2048]{2,1,0:T(8,128)(2,1)}, u32[]{:S(2)}) copy-start(bf16[16,24,2048]{2,1,0:T(8,128)(2,1)} %param.15) | copy-start | bytes 4718596
  7.2 19.8 %copy-start.2 = (bf16[128,2048]{1,0:T(8,128)(2,1)S(1)}, bf16[128,2048]{1,0:T(8,128)(2,1)}, u32[]{:S(2)}) copy-start(bf16[128,2048]{1,0:T(8,128)(2,1)} %param.10) | copy-start | bytes 1572868
  15.8 23.8 %all-to-all-start = ((bf16[32,1,10]{2,1,0:T(2,128)(2,1)}), bf16[32,1,10]{2,1,0:T(2,128)(2,1)S(1)}, u32[]{:S(2)}, u32[]{:S(2)}) async-start(bf16[32,1,10]{2,1,0:T(2,128)(2,1)} %all_to_all.53), calls=%async_computation | async-start | bytes 32768 | tf_op jit(solution)/shard_map/all_to_all | solution.py:75
  29.4 1.6 copy-start.3
  96.0 8.8 %copy-start.9 = (s32[32]{0:T(128)S(1)}, s32[32]{0:T(128)}, u32[]{:S(2)}) copy-start(s32[32]{0:T(128)} %param.14) | copy-start | bytes 388
  96.0 57.5 %all-to-all-start.3 = ((bf16[32,10,2048]{2,1,0:T(8,128)(2,1)}), bf16[32,10,2048]{2,1,0:T(8,128)(2,1)}, u32[]{:S(2)}, u32[]{:S(2)}) async-start(bf16[32,10,2048]{2,1,0:T(8,128)(2,1)} %get-tuple-element.30), calls=%async_computation.3 | async-start | bytes 4194304 | tf_op jit(solution)/shard_map/all_to_all | solution.py:73
  104.9 2.4 copy-start.6
  107.3 2.4 copy-start.7
  153.5 77.1 %copy-start.5 = (bf16[32,24,2048]{2,1,0:T(8,128)(2,1)S(1)}, bf16[32,24,2048]{2,1,0:T(8,128)(2,1)}, u32[]{:S(2)}) copy-start(bf16[32,24,2048]{2,1,0:T(8,128)(2,1)} %get-tuple-element.35) | copy-start | bytes 9437188
  308.7 81.8 %all-to-all-start.4 = ((bf16[32,24,2048]{2,1,0:T(8,128)(2,1)}), bf16[32,24,2048]{2,1,0:T(8,128)(2,1)}, u32[]{:S(2)}, u32[]{:S(2)}) async-start(bf16[32,24,2048]{2,1,0:T(8,128)(2,1)} %get-tuple-element.33), calls=%async_computation.4 | async-start | bytes 6291456 | tf_op jit(solution)/shard_map/all_to_all | solution.py:69
  317.2 403.4 %reduce-scatter.2.cloned.1.call-start = ((), (), s32[]{:S(2)}) async-start(), calls=%async_computation.10 | async-start | bytes 5308416 | tf_op jit(solution)/shard_map/reduce_scatter | solution.py:114
  329.7 4.3 copy-start.4
  398.0 3.5 copy-start.8
  635.2 17.1 %all-to-all-start.7 = ((bf16[32,1,10]{2,1,0:T(2,128)(2,1)}), bf16[32,1,10]{2,1,0:T(2,128)(2,1)S(1)}, u32[]{:S(2)}, u32[]{:S(2)}) async-start(bf16[32,1,10]{2,1,0:T(2,128)(2,1)} %convert_element_type.111), calls=%async_computation.7 | async-start | bytes 32768 | tf_op jit(solution)/shard_map/all_to_all | solution.py:94
  652.2 58.1 %all-to-all-start.6 = ((bf16[32,10,2048]{2,1,0:T(8,128)(2,1)}), bf16[32,10,2048]{2,1,0:T(8,128)(2,1)}, u32[]{:S(2)}, u32[]{:S(2)}) async-start(bf16[32,10,2048]{2,1,0:T(8,128)(2,1)} %reshape.160), calls=%async_computation.6 | async-start | bytes 4194304 | tf_op jit(solution)/shard_map/all_to_all | solution.py:87
  712.9 11.2 %copy-start.1 = (bf16[16,24,2048]{2,1,0:T(8,128)(2,1)S(1)}, bf16[16,24,2048]{2,1,0:T(8,128)(2,1)}, u32[]{:S(2)}) copy-start(bf16[16,24,2048]{2,1,0:T(8,128)(2,1)} %param.15) | copy-start | bytes 4718596
Sparse Core Ops, SparseCore 0:
  630.5 39.3 reduce-scatter.1
where the time goes:
time: 733 us; the launch traced here: 731 us
  blocking collectives  422 us (58%)
  waiting for transfers between devices  136 us (19%)
  local copies, waits for them, and re-layouts  46.4 us (6%)
  starting transfers between devices  46.2 us (6%)
  matrix products  38.3 us (5%)
  other arithmetic  28.3 us (4%)
  between operations  14.4 us (2%)
    all_to_all x1, blocking collectives, on_device(): lax.all_to_all(slot_parts, 'expert', split_axis=1, concat_axis=1, tiled=T...  210 us
    all_to_all x1, blocking collectives, on_device(): lax.all_to_all(wanted_down, 'expert', split_axis=0, concat_axis=1, tiled=...  78 us
    all_to_all x1, blocking collectives, on_device(): lax.all_to_all(wanted_gate, 'expert', split_axis=0, concat_axis=1, tiled=...  77.1 us
    all_to_all x1, blocking collectives, on_device(): lax.all_to_all(send_cot, 'expert', split_axis=0, concat_axis=0, tiled=True)  56.5 us
    all_to_all x1, waiting for transfers between devices, on_device(): lax.all_to_all(wanted_up, 'expert', split_axis=0, concat_axis=1, tiled=True)  54.3 us
    all_to_all x1, waiting for transfers between devices, on_device(): lax.all_to_all(pair_grad.reshape(slot_count, capacity, model_width), 'exp...  46.2 us
    all_to_all x1, waiting for transfers between devices, on_device(): lax.all_to_all(send_tokens, 'expert', split_axis=0, concat_axis=0, tiled=...  34.6 us
  transfers between devices with their start and end apart: 6, of which 4 were waited for; matrix products, arithmetic and copies ran while one was open for 10% of the time, Pallas kernels for 0%

commit v1 on v0

v1 whole, which is shorter than its diff:
```python
import functools

import jax
import jax.numpy as jnp
from jax import lax
from jax.experimental import pallas as pl
from jax.experimental.pallas import tpu as pltpu
from jax.sharding import PartitionSpec as P

F32 = jnp.float32
BF16 = jnp.bfloat16
I32 = jnp.int32
CAPACITY = 10
MAIN = 8
LANES = 128


def params():
    return pltpu.CompilerParams(vmem_limit_bytes=50 * 1024 * 1024)


def iota(shape, dim):
    return lax.broadcasted_iota(I32, shape, dim)


def ones_where(mask):
    return jnp.where(mask, 1.0, 0.0).astype(BF16)


def matmul(a, b):
    return jnp.dot(a, b, preferred_element_type=F32)


def matmul_t(a, b):
    return lax.dot_general(a, b, (((1,), (1,)), ((), ())), preferred_element_type=F32)


def pick_kernel(index_ref, gate_ref, up_ref, down_ref, out_ref):
    def one(slot, carry):
        expert = index_ref[1 + slot]
        out_ref[slot, 0] = gate_ref[expert]
        out_ref[slot, 1] = up_ref[expert]
        out_ref[slot, 2] = down_ref[expert]
        return carry

    lax.fori_loop(0, out_ref.shape[0], one, 0)


def pick(index, w_gate, w_up, w_down, slots, columns):
    experts, share, _ = w_gate.shape
    spec = pl.BlockSpec((experts, share, columns), lambda i, index: (0, 0, index[0]))
    return pl.pallas_call(
        pick_kernel,
        grid_spec=pltpu.PrefetchScalarGridSpec(
            num_scalar_prefetch=1,
            grid=(1,),
            in_specs=[spec] * 3,
            out_specs=pl.BlockSpec((slots, 3, share, columns), lambda i, index: (0, 0, 0, 0)),
        ),
        out_shape=jax.ShapeDtypeStruct((slots, 3, share, columns), BF16),
        compiler_params=params(),
    )(index, w_gate, w_up, w_down)


def pack_kernel(slots_ref, probs_ref, tok_ref, cot_ref, out_ref):
    tokens, width = tok_ref.shape
    count = out_ref.shape[0] // (2 * MAIN)
    quarter = width // 4
    first, second = slots_ref[0:1, :], slots_ref[1:2, :]
    row = iota((count, tokens), 0)
    in_first, in_second = first == row, second == row
    before = matmul(
        ones_where(in_first | in_second),
        ones_where(iota((tokens, tokens), 0) < iota((tokens, tokens), 1)),
    )
    rank_first = jnp.sum(jnp.where(in_first, before, 0.0), axis=0, keepdims=True).astype(I32)
    rank_second = jnp.sum(jnp.where(in_second, before, 0.0), axis=0, keepdims=True).astype(I32)
    code_first = first * 16 + rank_first
    code_second = second * 16 + rank_second

    row = iota((count * MAIN, tokens), 0)
    code = (row >> 3) * 16 + (row & 7)
    chosen = ones_where((code == code_first) | (code == code_second))
    for part in range(4):
        at = pl.ds(part * quarter, quarter)
        tok_rows = matmul(chosen, tok_ref[:, at]).reshape(count, MAIN, quarter)
        cot_rows = matmul(chosen, cot_ref[:, at]).reshape(count, MAIN, quarter)
        both = jnp.concatenate([tok_rows[:, None], cot_rows[:, None]], axis=1)
        out_ref[:, at] = both.reshape(count * 2 * MAIN, quarter).astype(BF16)

    row = iota((count * 2 * MAIN, tokens), 0)
    code = (row >> 4) * 16 + MAIN + (row & 1)
    hit = (code == code_first) | (code == code_second)
    total = jnp.zeros((count * 2 * MAIN, quarter), F32)
    for part in range(4):
        here = hit & (((row >> 2) & 3) == part)
        is_cot = ((row >> 1) & 1) == 1
        at = pl.ds(part * quarter, quarter)
        total += matmul(ones_where(here & jnp.logical_not(is_cot)), tok_ref[:, at])
        total += matmul(ones_where(here & is_cot), cot_ref[:, at])
    out_ref[:, pl.ds(width, quarter)] = total.astype(BF16)

    inner = row & 15
    rank = jnp.where(inner >= 8, inner - 8, jnp.where(inner < 2, inner + 8, 15))
    code = (row >> 4) * 16 + rank
    weight = jnp.sum(
        jnp.where(code == code_first, probs_ref[0:1, :], 0.0)
        + jnp.where(code == code_second, probs_ref[1:2, :], 0.0),
        axis=1,
        keepdims=True,
    )
    out_ref[:, pl.ds(width + quarter, LANES)] = jnp.broadcast_to(
        weight, (count * 2 * MAIN, LANES)
    ).astype(BF16)


def pack(slots_t, probs_t, tokens, cotangent, slots):
    width = tokens.shape[1]
    return pl.pallas_call(
        pack_kernel,
        out_shape=jax.ShapeDtypeStruct((slots * 2 * MAIN, width + width // 4 + LANES), BF16),
        compiler_params=params(),
    )(slots_t, probs_t, tokens, cotangent)


def hidden_kernel(
    main_ref, rest_ref, prob_ref, w_ref,
    part_ref, gate_grad_ref, up_grad_ref, hidden_ref, cot_ref,
    gate_acc, up_acc, down_acc, tok_keep, scaled_keep, weight_keep, gate_t, up_t, hidden_t,
):
    phase, step = pl.program_id(0), pl.program_id(1)
    rows = main_ref.shape[0]
    count = rows // 16
    mains, rests = count * MAIN, count * 2
    total = mains + rests
    columns = main_ref.shape[1]
    padded = tok_keep.shape[1]

    @pl.when((phase == 0) & (step == 0))
    def _():
        block = prob_ref[...].astype(F32).reshape(count, 2, MAIN, LANES)
        row, column = iota((rests, rows), 0), iota((rests, rows), 1)
        found = ones_where(column == (row >> 1) * 16 + (row & 1))
        weight_keep[0:mains, :] = block[:, 1].reshape(mains, LANES)
        weight_keep[mains:total, :] = matmul(found, prob_ref[...])
        gate_acc[...] = jnp.zeros_like(gate_acc)
        up_acc[...] = jnp.zeros_like(up_acc)
        down_acc[...] = jnp.zeros_like(down_acc)

    @pl.when(phase == 0)
    def _():
        block = main_ref[...].astype(F32).reshape(count, 2, MAIN, columns)
        row, column = iota((2 * rests, rows), 0), iota((2 * rests, rows), 1)
        is_cot = jnp.where(row >= rests, 1, 0)
        inner = row - is_cot * rests
        source = (inner >> 1) * 16 + (step // 2) * 4 + is_cot * 2 + (inner & 1)
        rest = matmul(ones_where(column == source), rest_ref[...])
        tok = jnp.concatenate([block[:, 0].reshape(mains, columns), rest[:rests]], axis=0).astype(BF16)
        cot = jnp.concatenate([block[:, 1].reshape(mains, columns), rest[rests:]], axis=0)
        scaled = (weight_keep[:, 0:1] * cot).astype(BF16)
        empty = jnp.zeros((padded - total, columns), BF16)
        tok_keep[step] = jnp.concatenate([tok, empty], axis=0)
        scaled_keep[step] = jnp.concatenate([scaled, empty], axis=0)
        cot_ref[0] = cot.astype(BF16)
        gate_acc[...] += matmul_t(tok, w_ref[0, 0])
        up_acc[...] += matmul_t(tok, w_ref[0, 1])
        down_acc[...] += matmul_t(scaled, w_ref[0, 2])

    @pl.when((phase == 1) & (step == 0))
    def _():
        hidden_units = gate_acc.shape[1]
        for start in range(0, padded, 128):
            size = min(128, total - start)
            at = pl.ds(start, size)
            gate_pre, up_pre, hidden_grad = gate_acc[at, :], up_acc[at, :], down_acc[at, :]
            sigma = jax.nn.sigmoid(gate_pre)
            swish = gate_pre * sigma
            hidden = swish * up_pre
            gate_grad = hidden_grad * up_pre * sigma * (1.0 + gate_pre * (1.0 - sigma))
            up_grad = hidden_grad * swish
            for value, out, out_t in (
                (hidden, hidden_ref, hidden_t),
                (gate_grad, gate_grad_ref, gate_t),
                (up_grad, up_grad_ref, up_t),
            ):
                out[at, :] = value.astype(BF16)
                if size < 128:
                    value = jnp.concatenate([value, jnp.zeros((128 - size, hidden_units), F32)], axis=0)
                out_t[:, pl.ds(start, 128)] = value.T.astype(BF16)

    @pl.when(phase == 1)
    def _():
        part_ref[0, 0] = matmul(gate_t[...], tok_keep[step]).astype(BF16)
        part_ref[0, 1] = matmul(up_t[...], tok_keep[step]).astype(BF16)
        part_ref[0, 2] = matmul(hidden_t[...], scaled_keep[step]).astype(BF16)


def hidden_layer(got, weights):
    steps, _, hidden, columns = weights.shape
    rows = got.shape[0]
    total = rows // 16 * CAPACITY
    padded = -(-total // 128) * 128
    width = steps * columns
    quarter = width // 4
    per_quarter = quarter // columns

    def held(shape):
        return pl.BlockSpec(shape, lambda phase, step: (0,) * len(shape))

    return pl.pallas_call(
        hidden_kernel,
        grid=(2, steps),
        in_specs=[
            pl.BlockSpec((rows, columns), lambda phase, step: (0, jnp.where(phase == 0, step, steps - 1))),
            pl.BlockSpec(
                (rows, columns),
                lambda phase, step: (0, jnp.where(phase == 0, steps + step % per_quarter, steps + per_quarter - 1)),
            ),
            pl.BlockSpec((rows, LANES), lambda phase, step: (0, (width + quarter) // LANES)),
            pl.BlockSpec(
                (1, 3, hidden, columns), lambda phase, step: (jnp.where(phase == 0, step, steps - 1), 0, 0, 0)
            ),
        ],
        out_specs=[
            pl.BlockSpec((1, 3, hidden, columns), lambda phase, step: (jnp.where(phase == 0, 0, step), 0, 0, 0)),
            held((total, hidden)),
            held((total, hidden)),
            held((total, hidden)),
            pl.BlockSpec((1, total, columns), lambda phase, step: (jnp.where(phase == 0, step, steps - 1), 0, 0)),
        ],
        out_shape=[
            jax.ShapeDtypeStruct((steps, 3, hidden, columns), BF16),
            jax.ShapeDtypeStruct((total, hidden), BF16),
            jax.ShapeDtypeStruct((total, hidden), BF16),
            jax.ShapeDtypeStruct((total, hidden), BF16),
            jax.ShapeDtypeStruct((steps, total, columns), BF16),
        ],
        scratch_shapes=[
            pltpu.VMEM((total, hidden), F32),
            pltpu.VMEM((total, hidden), F32),
            pltpu.VMEM((total, hidden), F32),
            pltpu.VMEM((steps, padded, columns), BF16),
            pltpu.VMEM((steps, padded, columns), BF16),
            pltpu.VMEM((total, LANES), F32),
            pltpu.VMEM((hidden, padded), BF16),
            pltpu.VMEM((hidden, padded), BF16),
            pltpu.VMEM((hidden, padded), BF16),
        ],
        compiler_params=params(),
    )(got, got, got, weights)


def pair_kernel(gate_grad_ref, up_grad_ref, hidden_ref, cot_ref, w_ref, out_ref, rest_acc, prob_acc):
    step = pl.program_id(0)
    steps = pl.num_programs(0)
    columns = w_ref.shape[3]
    mains = out_ref.shape[0]
    count = mains // MAIN
    rests = count * 2
    width = cot_ref.shape[2] * steps

    @pl.when(step == 0)
    def _():
        rest_acc[...] = jnp.zeros_like(rest_acc)
        prob_acc[...] = jnp.zeros_like(prob_acc)

    gate_w, up_w, down_w = w_ref[0, 0], w_ref[0, 1], w_ref[0, 2]
    grad = (matmul(gate_grad_ref[...], gate_w) + matmul(up_grad_ref[...], up_w)).astype(BF16)
    out_ref[:, pl.ds(pl.multiple_of(step * columns, columns), columns)] = grad[:mains]
    row, column = iota((mains, rests), 0), iota((mains, rests), 1)
    inner = row & 7
    placed = ones_where(((inner >> 1) == step // 2) & (column == (row >> 3) * 2 + (inner & 1)))
    rest_acc[step % 2] += matmul(placed, grad[mains:])
    prob_acc[...] += matmul(hidden_ref[...], down_w) * cot_ref[0].astype(F32)

    @pl.when(step == steps - 1)
    def _():
        out_ref[:, pl.ds(width, columns)] = rest_acc[0].astype(BF16)
        out_ref[:, pl.ds(width + columns, columns)] = rest_acc[1].astype(BF16)
        prob = jnp.broadcast_to(
            jnp.sum(prob_acc[...], axis=1, keepdims=True), (mains + rests, LANES)
        ).astype(BF16)
        placed = ones_where((inner < 2) & (column == (row >> 3) * 2 + inner))
        moved = matmul(placed, prob[mains:])
        lane = iota((mains, LANES), 1)
        out_ref[:, pl.ds(width + 2 * columns, LANES)] = jnp.where(
            lane < LANES // 2, prob[:mains].astype(F32), moved
        ).astype(BF16)


def pair_layer(gate_grad, up_grad, hidden, cot, weights):
    steps, _, units, columns = weights.shape
    total = gate_grad.shape[0]
    mains = total // CAPACITY * MAIN
    width = steps * columns
    lanes = width + width // 4 + LANES
    held = pl.BlockSpec((total, units), lambda step: (0, 0))
    return pl.pallas_call(
        pair_kernel,
        grid=(steps,),
        in_specs=[
            held,
            held,
            held,
            pl.BlockSpec((1, total, columns), lambda step: (step, 0, 0)),
            pl.BlockSpec((1, 3, units, columns), lambda step: (step, 0, 0, 0)),
        ],
        out_specs=pl.BlockSpec((mains, lanes), lambda step: (0, 0)),
        out_shape=jax.ShapeDtypeStruct((mains, lanes), BF16),
        scratch_shapes=[
            pltpu.VMEM((2, mains, columns), F32),
            pltpu.VMEM((total, columns), F32),
        ],
        compiler_params=params(),
    )(gate_grad, up_grad, hidden, cot, weights)


def combine_kernel(slots_ref, back_ref, token_ref, prob_ref):
    tokens, width = token_ref.shape
    mains = back_ref.shape[0]
    count = mains // MAIN
    quarter = width // 4
    first, second = slots_ref[:, 0:1], slots_ref[:, 1:2]
    column = iota((tokens, count), 1)
    in_first, in_second = first == column, second == column
    before = matmul(
        ones_where(iota((tokens, tokens), 0) > iota((tokens, tokens), 1)),
        ones_where(in_first | in_second),
    )
    rank_first = jnp.sum(jnp.where(in_first, before, 0.0), axis=1, keepdims=True).astype(I32)
    rank_second = jnp.sum(jnp.where(in_second, before, 0.0), axis=1, keepdims=True).astype(I32)
    code_first = first * 16 + rank_first
    code_second = second * 16 + rank_second

    cell = iota((tokens, mains), 1)
    code = (cell >> 3) * 16 + (cell & 7)
    main_first, main_second = code == code_first, code == code_second
    chosen = ones_where(main_first | main_second)
    code = (cell >> 3) * 16 + MAIN + (cell & 1)
    rest_hit = (code == code_first) | (code == code_second)
    rest_rows = back_ref[:, pl.ds(width, quarter)]
    for part in range(4):
        at = pl.ds(part * quarter, quarter)
        picked = ones_where(rest_hit & (((cell >> 1) & 3) == part))
        token_ref[:, at] = (matmul(chosen, back_ref[:, at]) + matmul(picked, rest_rows)).astype(BF16)

    probs = back_ref[:, pl.ds(width + quarter, LANES)]
    inner = cell & 7
    code = jnp.where(inner < 2, (cell >> 3) * 16 + MAIN + inner, -1)
    found = []
    for main_hit, mine in ((main_first, code_first), (main_second, code_second)):
        of_main = matmul(ones_where(main_hit), probs)[:, 0:1]
        of_rest = matmul(ones_where(code == mine), probs)[:, LANES // 2 : LANES // 2 + 1]
        found.append(of_main + of_rest)
    prob_ref[...] = jnp.concatenate(found, axis=1).astype(BF16)


def combine(routed_slots, back, tokens, width):
    return pl.pallas_call(
        combine_kernel,
        out_shape=[
            jax.ShapeDtypeStruct((tokens, width), BF16),
            jax.ShapeDtypeStruct((tokens, 2), BF16),
        ],
        compiler_params=params(),
    )(routed_slots, back)


def fold_kernel(placement_ref, part_ref, gate_ref, up_ref, down_ref, total):
    total[...] = jnp.zeros_like(total)

    def one(slot, carry):
        expert = placement_ref[slot]
        total[expert] += part_ref[slot].astype(F32)
        return carry

    lax.fori_loop(0, part_ref.shape[0], one, 0)
    gate_ref[...] = total[:, 0].astype(BF16)
    up_ref[...] = total[:, 1].astype(BF16)
    down_ref[...] = total[:, 2].astype(BF16)


def fold(placement, parts, experts):
    slots, _, share, columns = parts.shape
    spec = pl.BlockSpec((experts, share, columns), lambda i, placement: (0, 0, 0))
    return pl.pallas_call(
        fold_kernel,
        grid_spec=pltpu.PrefetchScalarGridSpec(
            num_scalar_prefetch=1,
            grid=(1,),
            in_specs=[pl.BlockSpec((slots, 3, share, columns), lambda i, placement: (0, 0, 0, 0))],
            out_specs=[spec] * 3,
            scratch_shapes=[pltpu.VMEM((experts, 3, share, columns), F32)],
        ),
        out_shape=[jax.ShapeDtypeStruct((experts, share, columns), BF16)] * 3,
        compiler_params=params(),
    )(placement, parts)


def over_expert(value):
    return lax.all_to_all(value, "expert", split_axis=0, concat_axis=0, tiled=True)


def on_device(tokens, cotangent, routed_slots, route_probs, placement, w_gate, w_up, w_down):
    slots = lax.axis_size("expert")
    groups = lax.axis_size("dp")
    token_rows, width = tokens.shape
    columns = width // groups
    experts, share, _ = w_gate.shape
    hidden = share * slots

    index = jnp.concatenate([lax.axis_index("dp").astype(I32)[None], placement])
    wanted = pick(index, w_gate, w_up, w_down, slots, columns)
    payload = pack(routed_slots.T, route_probs.T.astype(F32), tokens, cotangent, slots)
    mine = over_expert(wanted)
    mine, payload = lax.optimization_barrier((mine, payload))
    mine = mine.transpose(1, 0, 2, 3).reshape(3, hidden, columns)
    weights = lax.all_gather(mine, "dp", axis=0)
    got = over_expert(payload.reshape(slots, 2 * MAIN, -1)).reshape(payload.shape)

    parts, gate_grad, up_grad, hidden_rows, cot = hidden_layer(got, weights)
    summed = lax.psum_scatter(parts, "dp", scatter_dimension=0)
    pairs = pair_layer(gate_grad, up_grad, hidden_rows, cot, weights)
    back = over_expert(pairs.reshape(slots, MAIN, -1)).reshape(pairs.shape)
    token_grad, prob_grad = combine(routed_slots, back, token_rows, width)

    homeward = summed.reshape(3, slots, share, columns).transpose(1, 0, 2, 3)
    grads = fold(placement, over_expert(homeward), experts)
    return (token_grad, prob_grad, *grads)


def solution(mesh):
    placed = (
        P(("dp", "expert"), None),
        P(("dp", "expert"), None),
        P(("dp", "expert"), None),
        P(("dp", "expert"), None),
        P(),
        P(None, "expert", None),
        P(None, "expert", None),
        P(None, "expert", None),
    )
    return jax.shard_map(
        on_device,
        mesh=mesh,
        in_specs=placed,
        out_specs=(
            P(("dp", "expert"), None),
            P(("dp", "expert"), None),
            P(None, "expert", "dp"),
            P(None, "expert", "dp"),
            P(None, "expert", "dp"),
        ),
        check_vma=False,
    )
```

time: 733 us -> 256 us (0.35)
  blocking collectives: 422 us -> 69.8 us
  waiting for transfers between devices: 136 us -> 93.5 us
  Pallas kernels: 0 us -> 39 us
  local copies, waits for them, and re-layouts: 46.4 us -> 7.96 us
  matrix products: 38.3 us -> 0 us
  other arithmetic: 28.3 us -> 0.74 us
  starting transfers between devices: 46.2 us -> 29.3 us
    all_to_all x4 -> x1, blocking collectives: 422 us -> 69.8 us  [over_expert(): lax.all_to_all(value, 'expert', split_axis=0, concat_axis=0, tiled=True)]
    all_to_all x5 -> x3, waiting for transfers between devices: 136 us -> 53.6 us  [over_expert(): lax.all_to_all(value, 'expert', split_axis=0, concat_axis=0, tiled=True)]
    reduce_scatter x1, waiting for transfers between devices: 0.01 us -> 39.9 us  [on_device(): summed = lax.psum_scatter(parts, 'dp', scatter_dimension=0)]
    pallas_call x0 -> x6, Pallas kernels: none -> 39 us  [the longest x1 19 us: hidden_layer(): pl.pallas_call(hidden_kernel, grid=(2, steps), in_specs=[pl.BlockSpec((ro...]
    dot_general x10 -> x0, matrix products: 38.3 us -> none  [the longest x1 6.95 us: on_device(): jnp.einsum('es,gsfd->gefd', hosted.astype(jnp.bfloat16), home_parts, pref...]
    gather x10 -> x0, local copies, waits for them, and re-layouts: 22 us -> none  [the longest x2 4.07 us: on_device(): cotangent[row_index]]
    all_to_all x5 -> x3, starting transfers between devices: 46 us -> 29.3 us  [over_expert(): lax.all_to_all(value, 'expert', split_axis=0, concat_axis=0, tiled=True)]
    select_n x6 -> x0, other arithmetic: 11.3 us -> none  [the longest x1 6.7 us: on_device(): wanted_up = jnp.take(w_up, placement, axis=0)]
  transfers between devices with their start and end apart: 6 -> 5, of which waited for: 4 -> 3; matrix products, arithmetic and copies ran while one was open for 10% -> 1% of each run, Pallas kernels for 0% -> 6%
where the time goes in v1:
time: 256 us; the launch traced here: 255 us
  waiting for transfers between devices  93.5 us (37%)
  blocking collectives  69.8 us (27%)
  Pallas kernels  39 us (15%)
  starting transfers between devices  29.3 us (11%)
  between operations  14.1 us (6%)
  local copies, waits for them, and re-layouts  7.96 us (3%)
    all_to_all x1, blocking collectives, over_expert(): lax.all_to_all(value, 'expert', split_axis=0, concat_axis=0, tiled=True)  69.8 us
    all_to_all x3, waiting for transfers between devices, over_expert(): lax.all_to_all(value, 'expert', split_axis=0, concat_axis=0, tiled=True)  53.6 us
    reduce_scatter x1, waiting for transfers between devices, on_device(): summed = lax.psum_scatter(parts, 'dp', scatter_dimension=0)  39.9 us
    all_to_all x3, starting transfers between devices, over_expert(): lax.all_to_all(value, 'expert', split_axis=0, concat_axis=0, tiled=True)  29.3 us
    pallas_call x1, Pallas kernels, hidden_layer(): pl.pallas_call(hidden_kernel, grid=(2, steps), in_specs=[pl.BlockSpec((ro...  19 us
    pallas_call x1, Pallas kernels, pair_layer(): pl.pallas_call(pair_kernel, grid=(steps,), in_specs=[held, held, held, pl...  11.7 us
  transfers between devices with their start and end apart: 5, of which 3 were waited for; matrix products, arithmetic and copies ran while one was open for 1% of the time, Pallas kernels for 6%

profile of v1, /device:TPU:9, one launch (start us, length us, event | category | flops | bytes accessed | tf_op | source)
XLA Modules:
  0.0 254.5 jit_solution(15343058034980998067)
XLA Ops:
  7.2 0.7 pad_add_fusion.index_ref
  7.9 0.0 copy-start
  7.9 1.4 copy-done
  9.3 2.9 %shard_map.119 = bf16[32,3,24,256]{3,2,1,0:T(8,128)(2,1)} custom-call(s32[33]{0:T(128)S(1)} %pad_add_fusion.index_ref, bf16[16,24,2048]{2,1,0:T(8,128)(2,1)S(1)} %copy-done, bf16[16,24,2048]{2,1,0:T(8,128)(2,1)} %up_ref.1, bf16[16,24,2048]{2,1,0:T(8,128)(2,1)} %down_ref.1), custom_call_target="tpu_custom_call" | custom-call | tf_op jit(solution)/shard_map/pallas_call | solution.py:52
  12.2 0.0 copy-start.1
  12.2 11.3 %all-to-all-start = ((bf16[32,3,24,256]{3,2,1,0:T(8,128)(2,1)}), bf16[32,3,24,256]{3,2,1,0:T(8,128)(2,1)}, u32[]{:S(2)}, u32[]{:S(2)}) async-start(bf16[32,3,24,256]{3,2,1,0:T(8,128)(2,1)} %shard_map.119), calls=%async_computation | async-start | bytes 2359296 | tf_op jit(solution)/shard_map/all_to_all | solution.py:401
  23.5 0.0 all-gather.2.cloned.1.call-start
  23.5 0.0 copy-done.5
  23.6 0.0 copy-done.1
  23.6 0.0 copy-done.3
  23.6 0.0 copy-start.2
  23.6 1.0 copy-done.2
  24.6 2.0 shard_map.120
  26.6 24.4 %all-to-all-done = bf16[32,3,24,256]{3,2,1,0:T(8,128)(2,1)} async-done(((bf16[32,3,24,256]{3,2,1,0:T(8,128)(2,1)}), bf16[32,3,24,256]{3,2,1,0:T(8,128)(2,1)}, u32[]{:S(2)}, u32[]{:S(2)}) %all-to-all-start) | async-done | bytes 1179680 | tf_op jit(solution)/shard_map/all_to_all | solution.py:401
  51.0 2.4 copy.23
  53.4 0.0 all-gather.2.cloned.1.call-update
  53.4 0.0 reduce-scatter.2.cloned.1.call-start
  53.5 69.8 %all_to_all.20 = bf16[32,16,2688]{2,1,0:T(8,128)(2,1)} all-to-all(bf16[32,16,2688]{2,1,0:T(8,128)(2,1)S(1)} %bitcast.14), channel_id=1, replica_groups=mesh['dp'=8,'expert'=32] {'expert'}, dimensions={0} | all-to-all | bytes 5505024 | tf_op jit(solution)/shard_map/all_to_all | solution.py:401
  123.3 19.0 %shard_map.121 = (bf16[8,3,768,256]{3,2,1,0:T(8,128)(2,1)}, bf16[320,768]{1,0:T(8,128)(2,1)S(1)}, bf16[320,768]{1,0:T(8,128)(2,1)S(1)}, bf16[320,768]{1,0:T(8,128)(2,1)S(1)}, bf16[8,320,256]{2,1,0:T(8,128)(2,1)S(1)}) custom-call(bf16[512,2688]{1,0:T(8,128)(2,1)} %bitcast.17, bf16[512,2688]{1,0:T(8,128)(2,1)} %bitcast.18, bf16[512,2688]{1,0:T(8,128)(2,1)} %bitcast.19, ...), custom_call_target="tpu_custom_call" | custom-call | tf_op jit(solution)/shard_map/pallas_call | solution.py:210
  142.3 0.0 reduce-scatter.2.cloned.1.call-update
  142.3 11.7 %shard_map.122 = bf16[256,2688]{1,0:T(8,128)(2,1)} custom-call(bf16[320,768]{1,0:T(8,128)(2,1)S(1)} %get-tuple-element.19.gate_grad_ref, bf16[320,768]{1,0:T(8,128)(2,1)S(1)} %get-tuple-element.20.up_grad_ref, bf16[320,768]{1,0:T(8,128)(2,1)S(1)} %get-tuple-element.21.hidden_ref, bf16[8,320,256]{2,1,0:T(8,128)(2,1)S(1)} %get-tuple-element.22.cot_ref, ...), custom_call_target="tpu_custom_call" | custom-call | tf_op jit(solution)/shard_map/pallas_call | solution.py:298
  154.0 8.3 %all-to-all-start.2 = ((bf16[32,8,2688]{2,1,0:T(8,128)(2,1)}), bf16[32,8,2688]{2,1,0:T(8,128)(2,1)S(1)}, u32[]{:S(2)}, u32[]{:S(2)}) async-start(bf16[32,8,2688]{2,1,0:T(8,128)(2,1)} %bitcast.20), calls=%async_computation.2 | async-start | bytes 2752512 | tf_op jit(solution)/shard_map/all_to_all | solution.py:401
  162.3 39.9 %reduce-scatter.2.cloned.1.call-done = bf16[1,3,768,256]{3,2,1,0:T(8,128)(2,1)} async-done(((bf16[8,3,768,256]{3,2,1,0:T(8,128)(2,1)}), bf16[1,3,768,256]{3,2,1,0:T(8,128)(2,1)}) %reduce-scatter.2.cloned.1.call-update) | async-done | bytes 1179664 | tf_op jit(solution)/shard_map/reduce_scatter | solution.py:422
  202.2 2.4 copy.28
  204.6 0.0 all-to-all-done.2
  204.6 9.7 %all-to-all-start.3 = ((bf16[32,3,24,256]{3,2,1,0:T(8,128)(2,1)}), bf16[32,3,24,256]{3,2,1,0:T(8,128)(2,1)S(1)}, u32[]{:S(2)}, u32[]{:S(2)}) async-start(bf16[32,3,24,256]{3,2,1,0:T(8,128)(2,1)} %bitcast.21), calls=%async_computation.4 | async-start | bytes 2359296 | tf_op jit(solution)/shard_map/all_to_all | solution.py:401
  214.3 0.1 copy.24.slots_ref
  214.4 1.6 shard_map.123
  216.1 0.6 copy.26
  216.7 29.2 %all-to-all-done.3.part_ref = bf16[32,3,24,256]{3,2,1,0:T(8,128)(2,1)S(1)} async-done(((bf16[32,3,24,256]{3,2,1,0:T(8,128)(2,1)}), bf16[32,3,24,256]{3,2,1,0:T(8,128)(2,1)S(1)}, u32[]{:S(2)}, u32[]{:S(2)}) %all-to-all-start.3) | async-done | bytes 1179680 | tf_op jit(solution)/shard_map/all_to_all | solution.py:401
  245.8 0.0 copy-done.4
  245.8 1.8 shard_map.124
  (5 shorter events, 0.0 us)
Async XLA Ops:
  7.9 1.4 copy-start
  12.2 11.3 %copy-start.5 = (bf16[128,2]{0,1:T(2,128)(2,1)S(1)}, bf16[128,2]{0,1:T(2,128)(2,1)}, u32[]{:S(2)}) copy-start(bf16[128,2]{0,1:T(2,128)(2,1)} %param.11) | copy-start | bytes 1540
  12.2 11.4 %copy-start.1 = (bf16[128,2048]{1,0:T(8,128)(2,1)S(1)}, bf16[128,2048]{1,0:T(8,128)(2,1)}, u32[]{:S(2)}) copy-start(bf16[128,2048]{1,0:T(8,128)(2,1)} %tok_ref.1) | copy-start | bytes 1572868
  12.2 11.4 %copy-start.3 = (s32[128,2]{0,1:T(2,128)S(1)}, s32[128,2]{0,1:T(2,128)}, u32[]{:S(2)}) copy-start(s32[128,2]{0,1:T(2,128)} %param.10) | copy-start | bytes 3076
  12.2 38.8 %all-to-all-start = ((bf16[32,3,24,256]{3,2,1,0:T(8,128)(2,1)}), bf16[32,3,24,256]{3,2,1,0:T(8,128)(2,1)}, u32[]{:S(2)}, u32[]{:S(2)}) async-start(bf16[32,3,24,256]{3,2,1,0:T(8,128)(2,1)} %shard_map.119), calls=%async_computation | async-start | bytes 2359296 | tf_op jit(solution)/shard_map/all_to_all | solution.py:401
  23.5 99.8 %all-gather.2.cloned.1.call-start = ((), (), s32[]{:S(2)}) async-start(), calls=%async_computation.5 | async-start | bytes 10616832 | tf_op jit(solution)/shard_map/all_gather | solution.py:418
  23.6 1.0 copy-start.2
  53.4 148.8 %reduce-scatter.2.cloned.1.call-start = ((), (), s32[]{:S(2)}) async-start(), calls=%async_computation.6 | async-start | bytes 10616832 | tf_op jit(solution)/shard_map/reduce_scatter | solution.py:422
  154.0 50.6 %all-to-all-start.2 = ((bf16[32,8,2688]{2,1,0:T(8,128)(2,1)}), bf16[32,8,2688]{2,1,0:T(8,128)(2,1)S(1)}, u32[]{:S(2)}, u32[]{:S(2)}) async-start(bf16[32,8,2688]{2,1,0:T(8,128)(2,1)} %bitcast.20), calls=%async_computation.2 | async-start | bytes 2752512 | tf_op jit(solution)/shard_map/all_to_all | solution.py:401
  204.6 41.2 %copy-start.4 = (s32[32]{0:T(128)S(1)}, s32[32]{0:T(128)}, u32[]{:S(2)}) copy-start(s32[32]{0:T(128)} %placement_ref.1) | copy-start | bytes 388
  204.6 41.2 %all-to-all-start.3 = ((bf16[32,3,24,256]{3,2,1,0:T(8,128)(2,1)}), bf16[32,3,24,256]{3,2,1,0:T(8,128)(2,1)S(1)}, u32[]{:S(2)}, u32[]{:S(2)}) async-start(bf16[32,3,24,256]{3,2,1,0:T(8,128)(2,1)} %bitcast.21), calls=%async_computation.4 | async-start | bytes 2359296 | tf_op jit(solution)/shard_map/all_to_all | solution.py:401
Sparse Core Ops, SparseCore 0:
  53.5 57.1 all-gather.1
  142.4 59.7 reduce-scatter.1

commit v2 on v1

v2 whole, which is shorter than its diff:
```python
import functools

import jax
import jax.numpy as jnp
from jax import lax
from jax.experimental import pallas as pl
from jax.experimental.pallas import tpu as pltpu
from jax.sharding import PartitionSpec as P

F32 = jnp.float32
BF16 = jnp.bfloat16
I32 = jnp.int32
CAPACITY = 10
MAIN = 8
LANES = 128


def params():
    return pltpu.CompilerParams(vmem_limit_bytes=50 * 1024 * 1024)


def iota(shape, dim):
    return lax.broadcasted_iota(I32, shape, dim)


def ones_where(mask):
    return jnp.where(mask, 1.0, 0.0).astype(BF16)


def matmul(a, b):
    return jnp.dot(a, b, preferred_element_type=F32)


def matmul_t(a, b):
    return lax.dot_general(a, b, (((1,), (1,)), ((), ())), preferred_element_type=F32)


def pick_kernel(index_ref, gate_ref, up_ref, down_ref, out_ref):
    def one(slot, carry):
        expert = index_ref[1 + slot]
        out_ref[slot, 0] = gate_ref[expert]
        out_ref[slot, 1] = up_ref[expert]
        out_ref[slot, 2] = down_ref[expert]
        return carry

    lax.fori_loop(0, out_ref.shape[0], one, 0)


def pick(index, w_gate, w_up, w_down, slots, columns):
    experts, share, _ = w_gate.shape
    spec = pl.BlockSpec((experts, share, columns), lambda i, index: (0, 0, index[0]))
    return pl.pallas_call(
        pick_kernel,
        grid_spec=pltpu.PrefetchScalarGridSpec(
            num_scalar_prefetch=1,
            grid=(1,),
            in_specs=[spec] * 3,
            out_specs=pl.BlockSpec((slots, 3, share, columns), lambda i, index: (0, 0, 0, 0)),
        ),
        out_shape=jax.ShapeDtypeStruct((slots, 3, share, columns), BF16),
        compiler_params=params(),
    )(index, w_gate, w_up, w_down)


def pack_kernel(slots_ref, probs_ref, tok_ref, cot_ref, out_ref):
    tokens, width = tok_ref.shape
    count = out_ref.shape[0] // (2 * MAIN)
    quarter = width // 4
    first, second = slots_ref[0:1, :], slots_ref[1:2, :]
    row = iota((count, tokens), 0)
    in_first, in_second = first == row, second == row
    before = matmul(
        ones_where(in_first | in_second),
        ones_where(iota((tokens, tokens), 0) < iota((tokens, tokens), 1)),
    )
    rank_first = jnp.sum(jnp.where(in_first, before, 0.0), axis=0, keepdims=True).astype(I32)
    rank_second = jnp.sum(jnp.where(in_second, before, 0.0), axis=0, keepdims=True).astype(I32)
    code_first = first * 16 + rank_first
    code_second = second * 16 + rank_second

    def look_up(code):
        hit_first, hit_second = code == code_first, code == code_second
        weight = jnp.sum(
            jnp.where(hit_first, probs_ref[0:1, :], 0.0) + jnp.where(hit_second, probs_ref[1:2, :], 0.0),
            axis=1,
            keepdims=True,
        )
        return hit_first | hit_second, weight

    row = iota((count * MAIN, tokens), 0)
    hit, weight = look_up((row >> 3) * 16 + (row & 7))
    chosen = ones_where(hit)
    for part in range(4):
        at = pl.ds(part * quarter, quarter)
        tok_rows = matmul(chosen, tok_ref[:, at]).reshape(count, MAIN, quarter)
        cot_rows = (weight * matmul(chosen, cot_ref[:, at])).reshape(count, MAIN, quarter)
        both = jnp.concatenate([tok_rows[:, None], cot_rows[:, None]], axis=1)
        out_ref[:, at] = both.reshape(count * 2 * MAIN, quarter).astype(BF16)

    row = iota((count * 2 * MAIN, tokens), 0)
    hit, weight = look_up((row >> 4) * 16 + MAIN + (row & 1))
    is_cot = ((row >> 1) & 1) == 1
    tok_rows = jnp.zeros((count * 2 * MAIN, quarter), F32)
    cot_rows = jnp.zeros((count * 2 * MAIN, quarter), F32)
    for part in range(4):
        here = hit & (((row >> 2) & 3) == part)
        at = pl.ds(part * quarter, quarter)
        tok_rows += matmul(ones_where(here & jnp.logical_not(is_cot)), tok_ref[:, at])
        cot_rows += matmul(ones_where(here & is_cot), cot_ref[:, at])
    out_ref[:, pl.ds(width, quarter)] = (tok_rows + weight * cot_rows).astype(BF16)


def pack(slots_t, probs_t, tokens, cotangent, slots):
    width = tokens.shape[1]
    return pl.pallas_call(
        pack_kernel,
        out_shape=jax.ShapeDtypeStruct((slots * 2 * MAIN, width + width // 4), BF16),
        compiler_params=params(),
    )(slots_t, probs_t, tokens, cotangent)


def hidden_kernel(
    got_ref, w_ref,
    part_ref, gate_grad_ref, up_grad_ref, hidden_ref, scaled_ref,
    got_buf, rest_buf, w_buf, part_buf, tok_keep, scaled_keep, gate_acc, up_acc, down_acc, gate_t, up_t, hidden_t,
    got_sem, rest_sem, w_sem, part_sem,
):
    steps, rows, columns = got_buf.shape
    count = rows // 16
    mains, rests = count * MAIN, count * 2
    total = mains + rests
    padded = tok_keep.shape[1]
    units = gate_acc.shape[1]
    width = steps * columns

    rest_copy = pltpu.make_async_copy(got_ref.at[:, pl.ds(width, width // 4)], rest_buf, rest_sem)
    rest_copy.start()
    got_copies, w_copies = [], []
    for step in range(steps):
        got_copies.append(
            pltpu.make_async_copy(got_ref.at[:, pl.ds(step * columns, columns)], got_buf.at[step], got_sem.at[step])
        )
        w_copies.append(pltpu.make_async_copy(w_ref.at[step], w_buf.at[step], w_sem.at[step]))
        got_copies[step].start()
        w_copies[step].start()

    row, column = iota((2 * rests, rows), 0), iota((2 * rests, rows), 1)
    second = jnp.where(row >= rests, 1, 0)
    inner = row - second * rests
    source = (inner >> 1) * 16 + second * 2 + (inner & 1)
    rest_copy.wait()
    per_quarter = width // 4 // columns
    empty = jnp.zeros((padded - total, columns), BF16)
    for step in range(steps):
        got_copies[step].wait()
        block = got_buf[step].astype(F32).reshape(count, 2, MAIN, columns)
        found = ones_where(column == source + 4 * (step // per_quarter))
        rest = matmul(found, rest_buf[:, pl.ds(step % per_quarter * columns, columns)])
        tok = jnp.concatenate([block[:, 0].reshape(mains, columns), rest[:rests]], axis=0).astype(BF16)
        scaled = jnp.concatenate([block[:, 1].reshape(mains, columns), rest[rests:]], axis=0).astype(BF16)
        tok_keep[step, 0:total] = tok
        tok_keep[step, total:padded] = empty
        scaled_keep[step, 0:total] = scaled
        scaled_keep[step, total:padded] = empty
        scaled_ref[step] = scaled
        w_copies[step].wait()
        terms = (
            (gate_acc, matmul_t(tok, w_buf[step, 0])),
            (up_acc, matmul_t(tok, w_buf[step, 1])),
            (down_acc, matmul_t(scaled, w_buf[step, 2])),
        )
        for acc, term in terms:
            acc[...] = term if step == 0 else acc[...] + term

    for start in range(0, padded, 128):
        size = min(128, total - start)
        at = pl.ds(start, size)
        gate_pre, up_pre, hidden_grad = gate_acc[at, :], up_acc[at, :], down_acc[at, :]
        sigma = jax.nn.sigmoid(gate_pre)
        swish = gate_pre * sigma
        hidden = swish * up_pre
        gate_grad = hidden_grad * up_pre * sigma * (1.0 + gate_pre * (1.0 - sigma))
        up_grad = hidden_grad * swish
        for value, out, out_t in (
            (hidden, hidden_ref, hidden_t),
            (gate_grad, gate_grad_ref, gate_t),
            (up_grad, up_grad_ref, up_t),
        ):
            out[at, :] = value.astype(BF16)
            if size < 128:
                value = jnp.concatenate([value, jnp.zeros((128 - size, units), F32)], axis=0)
            out_t[:, pl.ds(start, 128)] = value.T.astype(BF16)

    part_copies = []
    slots, share = part_buf.shape[1], part_buf.shape[3]
    for step in range(steps):
        for matrix, (left, right) in enumerate(((gate_t, tok_keep), (up_t, tok_keep), (hidden_t, scaled_keep))):
            part = matmul(left[...], right[step])
            part_buf[step, :, matrix] = part.reshape(slots, share, columns).astype(BF16)
        part_copies.append(pltpu.make_async_copy(part_buf.at[step], part_ref.at[step], part_sem.at[step]))
        part_copies[step].start()
    for copy in part_copies:
        copy.wait()


def hidden_layer(got, weights, slots):
    steps, _, units, columns = weights.shape
    rows = got.shape[0]
    total = rows // 16 * CAPACITY
    padded = -(-total // 128) * 128
    width = steps * columns
    far = pl.BlockSpec(memory_space=pltpu.MemorySpace.HBM)
    near = pl.BlockSpec(memory_space=pltpu.VMEM)
    part_shape = (steps, slots, 3, units // slots, columns)
    return pl.pallas_call(
        hidden_kernel,
        in_specs=[pl.BlockSpec(memory_space=pl.ANY), far],
        out_specs=[far, near, near, near, near],
        out_shape=[
            jax.ShapeDtypeStruct(part_shape, BF16),
            jax.ShapeDtypeStruct((total, units), BF16),
            jax.ShapeDtypeStruct((total, units), BF16),
            jax.ShapeDtypeStruct((total, units), BF16),
            jax.ShapeDtypeStruct((steps, total, columns), BF16),
        ],
        scratch_shapes=[
            pltpu.VMEM((steps, rows, columns), BF16),
            pltpu.VMEM((rows, width // 4), BF16),
            pltpu.VMEM(weights.shape, BF16),
            pltpu.VMEM(part_shape, BF16),
            pltpu.VMEM((steps, padded, columns), BF16),
            pltpu.VMEM((steps, padded, columns), BF16),
            pltpu.VMEM((total, units), F32),
            pltpu.VMEM((total, units), F32),
            pltpu.VMEM((total, units), F32),
            pltpu.VMEM((units, padded), BF16),
            pltpu.VMEM((units, padded), BF16),
            pltpu.VMEM((units, padded), BF16),
            pltpu.SemaphoreType.DMA((steps,)),
            pltpu.SemaphoreType.DMA,
            pltpu.SemaphoreType.DMA((steps,)),
            pltpu.SemaphoreType.DMA((steps,)),
        ],
        compiler_params=params(),
    )(got, weights)


def pair_kernel(gate_grad_ref, up_grad_ref, hidden_ref, scaled_ref, w_ref, out_ref, w_buf, w_sem):
    steps, _, units, columns = w_buf.shape
    mains = out_ref.shape[0]
    count = mains // MAIN
    rests = count * 2
    width = steps * columns
    per_quarter = width // 4 // columns
    copies = [pltpu.make_async_copy(w_ref.at[step], w_buf.at[step], w_sem.at[step]) for step in range(steps)]
    for copy in copies:
        copy.start()

    row, column = iota((mains, rests), 0), iota((mains, rests), 1)
    inner = row & 7
    rest_sums = [None] * per_quarter
    dots = None
    for step in range(steps):
        copies[step].wait()
        grad = matmul(gate_grad_ref[...], w_buf[step, 0]) + matmul(up_grad_ref[...], w_buf[step, 1])
        grad = grad.astype(BF16)
        out_ref[:, pl.ds(step * columns, columns)] = grad[:mains]
        placed = ones_where(((inner >> 1) == step // per_quarter) & (column == (row >> 3) * 2 + (inner & 1)))
        moved = matmul(placed, grad[mains:])
        which = step % per_quarter
        rest_sums[which] = moved if rest_sums[which] is None else rest_sums[which] + moved
        term = matmul(hidden_ref[...], w_buf[step, 2]) * scaled_ref[step].astype(F32)
        dots = term if dots is None else dots + term

    for which in range(per_quarter):
        out_ref[:, pl.ds(width + which * columns, columns)] = rest_sums[which].astype(BF16)
    dots = jnp.broadcast_to(jnp.sum(dots, axis=1, keepdims=True), (mains + rests, LANES)).astype(BF16)
    moved = matmul(ones_where((inner < 2) & (column == (row >> 3) * 2 + inner)), dots[mains:])
    lane = iota((mains, LANES), 1)
    out_ref[:, pl.ds(width + width // 4, LANES)] = jnp.where(
        lane < LANES // 2, dots[:mains].astype(F32), moved
    ).astype(BF16)


def pair_layer(gate_grad, up_grad, hidden, scaled, weights):
    steps, _, units, columns = weights.shape
    mains = gate_grad.shape[0] // CAPACITY * MAIN
    width = steps * columns
    near = pl.BlockSpec(memory_space=pltpu.VMEM)
    return pl.pallas_call(
        pair_kernel,
        in_specs=[near, near, near, near, pl.BlockSpec(memory_space=pltpu.MemorySpace.HBM)],
        out_specs=near,
        out_shape=jax.ShapeDtypeStruct((mains, width + width // 4 + LANES), BF16),
        scratch_shapes=[pltpu.VMEM(weights.shape, BF16), pltpu.SemaphoreType.DMA((steps,))],
        compiler_params=params(),
    )(gate_grad, up_grad, hidden, scaled, weights)


def combine_kernel(slots_ref, weights_ref, back_ref, token_ref, prob_ref):
    tokens, width = token_ref.shape
    mains = back_ref.shape[0]
    count = mains // MAIN
    quarter = width // 4
    first, second = slots_ref[:, 0:1], slots_ref[:, 1:2]
    column = iota((tokens, count), 1)
    in_first, in_second = first == column, second == column
    before = matmul(
        ones_where(iota((tokens, tokens), 0) > iota((tokens, tokens), 1)),
        ones_where(in_first | in_second),
    )
    rank_first = jnp.sum(jnp.where(in_first, before, 0.0), axis=1, keepdims=True).astype(I32)
    rank_second = jnp.sum(jnp.where(in_second, before, 0.0), axis=1, keepdims=True).astype(I32)
    code_first = first * 16 + rank_first
    code_second = second * 16 + rank_second

    cell = iota((tokens, mains), 1)
    code = (cell >> 3) * 16 + (cell & 7)
    main_first, main_second = code == code_first, code == code_second
    chosen = ones_where(main_first | main_second)
    code = (cell >> 3) * 16 + MAIN + (cell & 1)
    rest_hit = (code == code_first) | (code == code_second)
    rest_rows = back_ref[:, pl.ds(width, quarter)]
    for part in range(4):
        at = pl.ds(part * quarter, quarter)
        picked = ones_where(rest_hit & (((cell >> 1) & 3) == part))
        token_ref[:, at] = (matmul(chosen, back_ref[:, at]) + matmul(picked, rest_rows)).astype(BF16)

    probs = back_ref[:, pl.ds(width + quarter, LANES)]
    inner = cell & 7
    code = jnp.where(inner < 2, (cell >> 3) * 16 + MAIN + inner, -1)
    found = []
    for main_hit, mine in ((main_first, code_first), (main_second, code_second)):
        of_main = matmul(ones_where(main_hit), probs)[:, 0:1]
        of_rest = matmul(ones_where(code == mine), probs)[:, LANES // 2 : LANES // 2 + 1]
        found.append(of_main + of_rest)
    prob_ref[...] = (jnp.concatenate(found, axis=1) / weights_ref[...].astype(F32)).astype(BF16)


def combine(routed_slots, route_probs, back, tokens, width):
    return pl.pallas_call(
        combine_kernel,
        out_shape=[
            jax.ShapeDtypeStruct((tokens, width), BF16),
            jax.ShapeDtypeStruct((tokens, 2), BF16),
        ],
        compiler_params=params(),
    )(routed_slots, route_probs, back)


def fold_kernel(placement_ref, part_ref, gate_ref, up_ref, down_ref, total):
    total[...] = jnp.zeros_like(total)

    def one(slot, carry):
        expert = placement_ref[slot]
        total[expert] += part_ref[slot].astype(F32)
        return carry

    lax.fori_loop(0, part_ref.shape[0], one, 0)
    gate_ref[...] = total[:, 0].astype(BF16)
    up_ref[...] = total[:, 1].astype(BF16)
    down_ref[...] = total[:, 2].astype(BF16)


def fold(placement, parts, experts):
    slots, _, share, columns = parts.shape
    spec = pl.BlockSpec((experts, share, columns), lambda i, placement: (0, 0, 0))
    return pl.pallas_call(
        fold_kernel,
        grid_spec=pltpu.PrefetchScalarGridSpec(
            num_scalar_prefetch=1,
            grid=(1,),
            in_specs=[pl.BlockSpec((slots, 3, share, columns), lambda i, placement: (0, 0, 0, 0))],
            out_specs=[spec] * 3,
            scratch_shapes=[pltpu.VMEM((experts, 3, share, columns), F32)],
        ),
        out_shape=[jax.ShapeDtypeStruct((experts, share, columns), BF16)] * 3,
        compiler_params=params(),
    )(placement, parts)


def over_expert(value):
    return lax.all_to_all(value, "expert", split_axis=0, concat_axis=0, tiled=True)


def on_device(tokens, cotangent, routed_slots, route_probs, placement, w_gate, w_up, w_down):
    slots = lax.axis_size("expert")
    groups = lax.axis_size("dp")
    token_rows, width = tokens.shape
    columns = width // groups
    experts, share, _ = w_gate.shape
    hidden = share * slots

    index = jnp.concatenate([lax.axis_index("dp").astype(I32)[None], placement])
    wanted = pick(index, w_gate, w_up, w_down, slots, columns)
    payload = pack(routed_slots.T, route_probs.T.astype(F32), tokens, cotangent, slots)
    mine = over_expert(wanted)
    mine, payload = lax.optimization_barrier((mine, payload))
    mine = mine.transpose(1, 0, 2, 3).reshape(3, hidden, columns)
    weights = lax.all_gather(mine, "dp", axis=0)
    got = over_expert(payload.reshape(slots, 2 * MAIN, -1)).reshape(payload.shape)

    parts, gate_grad, up_grad, hidden_rows, scaled = hidden_layer(got, weights, slots)
    summed = lax.psum_scatter(parts, "dp", scatter_dimension=0)
    pairs = pair_layer(gate_grad, up_grad, hidden_rows, scaled, weights)
    back = over_expert(pairs.reshape(slots, MAIN, -1)).reshape(pairs.shape)
    token_grad, prob_grad = combine(routed_slots, route_probs, back, token_rows, width)

    grads = fold(placement, over_expert(summed), experts)
    return (token_grad, prob_grad, *grads)


def solution(mesh):
    placed = (
        P(("dp", "expert"), None),
        P(("dp", "expert"), None),
        P(("dp", "expert"), None),
        P(("dp", "expert"), None),
        P(),
        P(None, "expert", None),
        P(None, "expert", None),
        P(None, "expert", None),
    )
    return jax.shard_map(
        on_device,
        mesh=mesh,
        in_specs=placed,
        out_specs=(
            P(("dp", "expert"), None),
            P(("dp", "expert"), None),
            P(None, "expert", "dp"),
            P(None, "expert", "dp"),
            P(None, "expert", "dp"),
        ),
        check_vma=False,
    )
```

time: 256 us -> 249 us (0.973)
  blocking collectives: 69.8 us -> 109 us
  waiting for transfers between devices: 93.5 us -> 60.9 us
  starting transfers between devices: 29.3 us -> 20.9 us
    all_to_all x1 -> x2, blocking collectives: 69.8 us -> 109 us  [over_expert(): lax.all_to_all(value, 'expert', split_axis=0, concat_axis=0, tiled=True)]
    reduce_scatter x1, waiting for transfers between devices: 39.9 us -> 7.48 us  [on_device(): summed = lax.psum_scatter(parts, 'dp', scatter_dimension=0)]
    all_to_all x3 -> x2, starting transfers between devices: 29.3 us -> 20.8 us  [over_expert(): lax.all_to_all(value, 'expert', split_axis=0, concat_axis=0, tiled=True)]
    all_to_all x3 -> x2, waiting for transfers between devices: 53.6 us -> 53.4 us  [over_expert(): lax.all_to_all(value, 'expert', split_axis=0, concat_axis=0, tiled=True)]
  transfers between devices with their start and end apart: 5 -> 4, of which waited for: 3 -> 3; matrix products, arithmetic and copies ran while one was open for 1% -> 0% of each run, Pallas kernels for 6% -> 6%
where the time goes in v2:
time: 249 us; the launch traced here: 248 us
  blocking collectives  109 us (44%)
  waiting for transfers between devices  60.9 us (24%)
  Pallas kernels  36.9 us (15%)
  starting transfers between devices  20.9 us (8%)
  between operations  14.1 us (6%)
  local copies, waits for them, and re-layouts  5.69 us (2%)
    all_to_all x2, blocking collectives, over_expert(): lax.all_to_all(value, 'expert', split_axis=0, concat_axis=0, tiled=True)  109 us
    all_to_all x2, waiting for transfers between devices, over_expert(): lax.all_to_all(value, 'expert', split_axis=0, concat_axis=0, tiled=True)  53.4 us
    all_to_all x2, starting transfers between devices, over_expert(): lax.all_to_all(value, 'expert', split_axis=0, concat_axis=0, tiled=True)  20.8 us
    pallas_call x1, Pallas kernels, hidden_layer(): pl.pallas_call(hidden_kernel, in_specs=[pl.BlockSpec(memory_space=pl.ANY)...  17.6 us
    pallas_call x1, Pallas kernels, pair_layer(): pl.pallas_call(pair_kernel, in_specs=[near, near, near, near, pl.BlockSpe...  10.9 us
    reduce_scatter x1, waiting for transfers between devices, on_device(): summed = lax.psum_scatter(parts, 'dp', scatter_dimension=0)  7.48 us
  transfers between devices with their start and end apart: 4, of which 3 were waited for; matrix products, arithmetic and copies ran while one was open for 0% of the time, Pallas kernels for 6%

profile of v2, /device:TPU:9, one launch (start us, length us, event | category | flops | bytes accessed | tf_op | source)
XLA Modules:
  0.0 247.7 jit_solution(13507963236154920650)
XLA Ops:
  7.2 0.7 pad_add_fusion.index_ref
  7.9 0.0 copy-start
  7.9 1.4 copy-done
  9.3 2.9 %shard_map.119 = bf16[32,3,24,256]{3,2,1,0:T(8,128)(2,1)} custom-call(s32[33]{0:T(128)S(1)} %pad_add_fusion.index_ref, bf16[16,24,2048]{2,1,0:T(8,128)(2,1)S(1)} %copy-done, bf16[16,24,2048]{2,1,0:T(8,128)(2,1)} %up_ref.1, bf16[16,24,2048]{2,1,0:T(8,128)(2,1)} %down_ref.1), custom_call_target="tpu_custom_call" | custom-call | tf_op jit(solution)/shard_map/pallas_call | solution.py:52
  12.2 0.0 copy-start.5
  12.2 11.3 %all-to-all-start = ((bf16[32,3,24,256]{3,2,1,0:T(8,128)(2,1)}), bf16[32,3,24,256]{3,2,1,0:T(8,128)(2,1)}, u32[]{:S(2)}, u32[]{:S(2)}) async-start(bf16[32,3,24,256]{3,2,1,0:T(8,128)(2,1)} %shard_map.119), calls=%async_computation | async-start | bytes 2359296 | tf_op jit(solution)/shard_map/all_to_all | solution.py:383
  23.5 0.0 all-gather.2.cloned.1.call-start
  23.5 0.0 copy-done.5
  23.6 0.0 copy-done.1
  23.6 0.0 copy-done.3
  23.6 0.0 copy-start.2
  23.6 1.0 copy-done.2
  24.6 2.1 shard_map.120
  26.7 24.3 %all-to-all-done = bf16[32,3,24,256]{3,2,1,0:T(8,128)(2,1)} async-done(((bf16[32,3,24,256]{3,2,1,0:T(8,128)(2,1)}), bf16[32,3,24,256]{3,2,1,0:T(8,128)(2,1)}, u32[]{:S(2)}, u32[]{:S(2)}) %all-to-all-start) | async-done | bytes 1179680 | tf_op jit(solution)/shard_map/all_to_all | solution.py:383
  51.0 2.4 copy.20
  53.4 0.0 all-gather.2.cloned.1.call-update
  53.4 0.0 reduce-scatter.2.cloned.1.call-start
  53.5 66.7 %all_to_all.20 = bf16[32,16,2560]{2,1,0:T(8,128)(2,1)} all-to-all(bf16[32,16,2560]{2,1,0:T(8,128)(2,1)S(1)} %bitcast.11), channel_id=1, replica_groups=mesh['dp'=8,'expert'=32] {'expert'}, dimensions={0} | all-to-all | bytes 5242880 | tf_op jit(solution)/shard_map/all_to_all | solution.py:383
  120.2 17.6 %shard_map.121 = (bf16[8,32,3,24,256]{4,3,2,1,0:T(8,128)(2,1)}, bf16[320,768]{1,0:T(8,128)(2,1)S(1)}, bf16[320,768]{1,0:T(8,128)(2,1)S(1)}, bf16[320,768]{1,0:T(8,128)(2,1)S(1)}, bf16[8,320,256]{2,1,0:T(8,128)(2,1)S(1)}) custom-call(bf16[512,2560]{1,0:T(8,128)(2,1)} %bitcast.14, bf16[8,3,768,256]{3,2,1,0:T(8,128)(2,1)} %all-gather.2.cloned.1.call-done.w_ref), custom_call_target="tpu_custom_call" | custom-call | tf_op jit(solution)/shard_map/pallas_call | solution.py:215
  137.8 0.0 reduce-scatter.2.cloned.1.call-update
  137.8 10.9 %shard_map.122 = bf16[256,2688]{1,0:T(8,128)(2,1)} custom-call(bf16[320,768]{1,0:T(8,128)(2,1)S(1)} %get-tuple-element.19.gate_grad_ref, bf16[320,768]{1,0:T(8,128)(2,1)S(1)} %get-tuple-element.20.up_grad_ref, bf16[320,768]{1,0:T(8,128)(2,1)S(1)} %get-tuple-element.21.hidden_ref, bf16[8,320,256]{2,1,0:T(8,128)(2,1)S(1)} %get-tuple-element.22.scaled_ref, ...), custom_call_target="tpu_custom_call" | custom-call | tf_op jit(solution)/shard_map/pallas_call | solution.py:290
  148.7 41.8 %all_to_all.21 = bf16[32,8,2688]{2,1,0:T(8,128)(2,1)S(1)} all-to-all(bf16[32,8,2688]{2,1,0:T(8,128)(2,1)} %bitcast.15), channel_id=1, replica_groups=mesh['dp'=8,'expert'=32] {'expert'}, dimensions={0} | all-to-all | bytes 2752512 | tf_op jit(solution)/shard_map/all_to_all | solution.py:383
  190.5 7.5 %reduce-scatter.2.cloned.1.call-done = bf16[1,32,3,24,256]{4,3,2,1,0:T(8,128)(2,1)} async-done(((bf16[8,32,3,24,256]{4,3,2,1,0:T(8,128)(2,1)}), bf16[1,32,3,24,256]{4,3,2,1,0:T(8,128)(2,1)}) %reduce-scatter.2.cloned.1.call-update) | async-done | bytes 1179664 | tf_op jit(solution)/shard_map/reduce_scatter | solution.py:404
  198.0 9.6 %all-to-all-start.3 = ((bf16[32,3,24,256]{3,2,1,0:T(8,128)(2,1)}), bf16[32,3,24,256]{3,2,1,0:T(8,128)(2,1)S(1)}, u32[]{:S(2)}, u32[]{:S(2)}) async-start(bf16[32,3,24,256]{3,2,1,0:T(8,128)(2,1)} %bitcast.17), calls=%async_computation.4 | async-start | bytes 2359296 | tf_op jit(solution)/shard_map/all_to_all | solution.py:383
  207.5 0.0 copy-start.4
  207.6 0.1 copy.21.slots_ref
  207.7 0.1 copy.22.weights_ref
  207.8 1.6 shard_map.123
  209.4 0.6 copy.23
  210.0 29.0 %all-to-all-done.3.part_ref = bf16[32,3,24,256]{3,2,1,0:T(8,128)(2,1)S(1)} async-done(((bf16[32,3,24,256]{3,2,1,0:T(8,128)(2,1)}), bf16[32,3,24,256]{3,2,1,0:T(8,128)(2,1)S(1)}, u32[]{:S(2)}, u32[]{:S(2)}) %all-to-all-start.3) | async-done | bytes 1179680 | tf_op jit(solution)/shard_map/all_to_all | solution.py:383
  239.1 0.0 copy-done.4
  239.1 1.8 shard_map.124
  (4 shorter events, 0.0 us)
Async XLA Ops:
  7.9 1.4 copy-start
  12.2 11.3 %copy-start.5 = (bf16[128,2]{0,1:T(2,128)(2,1)S(1)}, bf16[128,2]{0,1:T(2,128)(2,1)}, u32[]{:S(2)}) copy-start(bf16[128,2]{0,1:T(2,128)(2,1)} %param.11) | copy-start | bytes 1540
  12.2 11.4 %copy-start.1 = (bf16[128,2048]{1,0:T(8,128)(2,1)S(1)}, bf16[128,2048]{1,0:T(8,128)(2,1)}, u32[]{:S(2)}) copy-start(bf16[128,2048]{1,0:T(8,128)(2,1)} %tok_ref.1) | copy-start | bytes 1572868
  12.2 11.4 %copy-start.3 = (s32[128,2]{0,1:T(2,128)S(1)}, s32[128,2]{0,1:T(2,128)}, u32[]{:S(2)}) copy-start(s32[128,2]{0,1:T(2,128)} %param.10) | copy-start | bytes 3076
  12.2 38.8 %all-to-all-start = ((bf16[32,3,24,256]{3,2,1,0:T(8,128)(2,1)}), bf16[32,3,24,256]{3,2,1,0:T(8,128)(2,1)}, u32[]{:S(2)}, u32[]{:S(2)}) async-start(bf16[32,3,24,256]{3,2,1,0:T(8,128)(2,1)} %shard_map.119), calls=%async_computation | async-start | bytes 2359296 | tf_op jit(solution)/shard_map/all_to_all | solution.py:383
  23.5 96.7 %all-gather.2.cloned.1.call-start = ((), (), s32[]{:S(2)}) async-start(), calls=%async_computation.5 | async-start | bytes 10616832 | tf_op jit(solution)/shard_map/all_gather | solution.py:400
  23.6 1.0 copy-start.2
  53.4 144.6 %reduce-scatter.2.cloned.1.call-start = ((), (), s32[]{:S(2)}) async-start(), calls=%async_computation.6 | async-start | bytes 10616832 | tf_op jit(solution)/shard_map/reduce_scatter | solution.py:404
  198.0 41.1 %all-to-all-start.3 = ((bf16[32,3,24,256]{3,2,1,0:T(8,128)(2,1)}), bf16[32,3,24,256]{3,2,1,0:T(8,128)(2,1)S(1)}, u32[]{:S(2)}, u32[]{:S(2)}) async-start(bf16[32,3,24,256]{3,2,1,0:T(8,128)(2,1)} %bitcast.17), calls=%async_computation.4 | async-start | bytes 2359296 | tf_op jit(solution)/shard_map/all_to_all | solution.py:383
  207.5 31.5 %copy-start.4 = (s32[32]{0:T(128)S(1)}, s32[32]{0:T(128)}, u32[]{:S(2)}) copy-start(s32[32]{0:T(128)} %placement_ref.1) | copy-start | bytes 388
Sparse Core Ops, SparseCore 0:
  53.5 57.1 all-gather.1
  137.9 60.0 reduce-scatter.1

commit v3 on v2

--- a/solution.py
+++ b/solution.py
@@ -15,8 +15,16 @@
 LANES = 128
 
 
-def params():
-    return pltpu.CompilerParams(vmem_limit_bytes=50 * 1024 * 1024)
+def params(mib=20):
+    return pltpu.CompilerParams(vmem_limit_bytes=mib * 1024 * 1024)
+
+
+def far():
+    return pl.BlockSpec(memory_space=pltpu.MemorySpace.HBM)
+
+
+def near():
+    return pl.BlockSpec(memory_space=pltpu.VMEM)
 
 
 def iota(shape, dim):
@@ -35,31 +43,40 @@
     return lax.dot_general(a, b, (((1,), (1,)), ((), ())), preferred_element_type=F32)
 
 
-def pick_kernel(index_ref, gate_ref, up_ref, down_ref, out_ref):
-    def one(slot, carry):
-        expert = index_ref[1 + slot]
-        out_ref[slot, 0] = gate_ref[expert]
-        out_ref[slot, 1] = up_ref[expert]
-        out_ref[slot, 2] = down_ref[expert]
-        return carry
-
-    lax.fori_loop(0, out_ref.shape[0], one, 0)
-
-
-def pick(index, w_gate, w_up, w_down, slots, columns):
+def matmul_tt(a, b):
+    return lax.dot_general(a, b, (((0,), (1,)), ((), ())), preferred_element_type=F32)
+
+
+def pick_kernel(placement_ref, gate_ref, up_ref, down_ref, out_ref, buf, sem):
+    columns = out_ref.shape[3]
+    at = pl.ds(pl.multiple_of(lax.axis_index("dp") * columns, columns), columns)
+    copies = [
+        pltpu.make_async_copy(ref.at[:, :, at], buf.at[matrix], sem.at[matrix])
+        for matrix, ref in enumerate((gate_ref, up_ref, down_ref))
+    ]
+    for copy in copies:
+        copy.start()
+    for matrix, copy in enumerate(copies):
+        copy.wait()
+        for slot in range(out_ref.shape[0]):
+            out_ref[slot, matrix] = buf[matrix, placement_ref[slot]]
+
+
+def pick(placement, w_gate, w_up, w_down, slots, columns):
     experts, share, _ = w_gate.shape
-    spec = pl.BlockSpec((experts, share, columns), lambda i, index: (0, 0, index[0]))
     return pl.pallas_call(
         pick_kernel,
-        grid_spec=pltpu.PrefetchScalarGridSpec(
-            num_scalar_prefetch=1,
-            grid=(1,),
-            in_specs=[spec] * 3,
-            out_specs=pl.BlockSpec((slots, 3, share, columns), lambda i, index: (0, 0, 0, 0)),
-        ),
+        in_specs=[pl.BlockSpec(memory_space=pltpu.SMEM), far(), far(), far()],
+        out_specs=near(),
         out_shape=jax.ShapeDtypeStruct((slots, 3, share, columns), BF16),
-        compiler_params=params(),
-    )(index, w_gate, w_up, w_down)
+        scratch_shapes=[pltpu.VMEM((3, experts, share, columns), BF16), pltpu.SemaphoreType.DMA((3,))],
+        compiler_params=params(56),
+    )(placement, w_gate, w_up, w_down)
+
+
+def whole(block):
+    slots, share, columns = block.shape
+    return block.reshape(slots * share, columns)
 
 
 def pack_kernel(slots_ref, probs_ref, tok_ref, cot_ref, out_ref):
@@ -125,52 +142,63 @@
     got_buf, rest_buf, w_buf, part_buf, tok_keep, scaled_keep, gate_acc, up_acc, down_acc, gate_t, up_t, hidden_t,
     got_sem, rest_sem, w_sem, part_sem,
 ):
-    steps, rows, columns = got_buf.shape
+    quarters, rows, quarter = got_buf.shape
+    steps, slots, _, share, columns = w_buf.shape
+    units = slots * share
+    each = steps // quarters
     count = rows // 16
     mains, rests = count * MAIN, count * 2
     total = mains + rests
     padded = tok_keep.shape[1]
-    units = gate_acc.shape[1]
-    width = steps * columns
-
-    rest_copy = pltpu.make_async_copy(got_ref.at[:, pl.ds(width, width // 4)], rest_buf, rest_sem)
+
+    def got_copy(part):
+        at = pl.ds(pl.multiple_of(part * quarter, quarter), quarter)
+        return pltpu.make_async_copy(got_ref.at[:, at], got_buf.at[part], got_sem.at[part])
+
+    def w_copy(part):
+        at = pl.ds(part * each, each)
+        return pltpu.make_async_copy(w_ref.at[at], w_buf.at[at], w_sem.at[part])
+
+    rest_copy = pltpu.make_async_copy(got_ref.at[:, pl.ds(quarters * quarter, quarter)], rest_buf, rest_sem)
     rest_copy.start()
-    got_copies, w_copies = [], []
+    for part in range(2):
+        got_copy(part).start()
+        w_copy(part).start()
+    gate_acc[...] = jnp.zeros_like(gate_acc)
+    up_acc[...] = jnp.zeros_like(up_acc)
+    down_acc[...] = jnp.zeros_like(down_acc)
     for step in range(steps):
-        got_copies.append(
-            pltpu.make_async_copy(got_ref.at[:, pl.ds(step * columns, columns)], got_buf.at[step], got_sem.at[step])
-        )
-        w_copies.append(pltpu.make_async_copy(w_ref.at[step], w_buf.at[step], w_sem.at[step]))
-        got_copies[step].start()
-        w_copies[step].start()
-
+        tok_keep[step, total:padded] = jnp.zeros((padded - total, columns), BF16)
+        scaled_keep[step, total:padded] = jnp.zeros((padded - total, columns), BF16)
     row, column = iota((2 * rests, rows), 0), iota((2 * rests, rows), 1)
     second = jnp.where(row >= rests, 1, 0)
     inner = row - second * rests
-    source = (inner >> 1) * 16 + second * 2 + (inner & 1)
+    offset = column - (inner >> 1) * 16 - second * 2 - (inner & 1)
     rest_copy.wait()
-    per_quarter = width // 4 // columns
-    empty = jnp.zeros((padded - total, columns), BF16)
-    for step in range(steps):
-        got_copies[step].wait()
-        block = got_buf[step].astype(F32).reshape(count, 2, MAIN, columns)
-        found = ones_where(column == source + 4 * (step // per_quarter))
-        rest = matmul(found, rest_buf[:, pl.ds(step % per_quarter * columns, columns)])
-        tok = jnp.concatenate([block[:, 0].reshape(mains, columns), rest[:rests]], axis=0).astype(BF16)
-        scaled = jnp.concatenate([block[:, 1].reshape(mains, columns), rest[rests:]], axis=0).astype(BF16)
-        tok_keep[step, 0:total] = tok
-        tok_keep[step, total:padded] = empty
-        scaled_keep[step, 0:total] = scaled
-        scaled_keep[step, total:padded] = empty
-        scaled_ref[step] = scaled
-        w_copies[step].wait()
-        terms = (
-            (gate_acc, matmul_t(tok, w_buf[step, 0])),
-            (up_acc, matmul_t(tok, w_buf[step, 1])),
-            (down_acc, matmul_t(scaled, w_buf[step, 2])),
-        )
-        for acc, term in terms:
-            acc[...] = term if step == 0 else acc[...] + term
+
+    def forward(part, carry):
+        @pl.when(part + 2 < quarters)
+        def _():
+            got_copy(part + 2).start()
+            w_copy(part + 2).start()
+
+        got_copy(part).wait()
+        block = got_buf[part].astype(F32).reshape(count, 2, MAIN, quarter)
+        rest = matmul(ones_where(offset == part * 4), rest_buf[...])
+        tok = jnp.concatenate([block[:, 0].reshape(mains, quarter), rest[:rests]], axis=0).astype(BF16)
+        scaled = jnp.concatenate([block[:, 1].reshape(mains, quarter), rest[rests:]], axis=0).astype(BF16)
+        for i in range(each):
+            at = slice(i * columns, (i + 1) * columns)
+            tok_keep[part * each + i, 0:total] = tok[:, at]
+            scaled_keep[part * each + i, 0:total] = scaled[:, at]
+            scaled_ref[part * each + i] = scaled[:, at]
+        w_copy(part).wait()
+        for acc, left, matrix in ((gate_acc, tok, 0), (up_acc, tok, 1), (down_acc, scaled, 2)):
+            right = jnp.concatenate([whole(w_buf[part * each + i, :, matrix]) for i in range(each)], axis=1)
+            acc[...] += matmul_t(left, right)
+        return carry
+
+    lax.fori_loop(0, quarters, forward, 0)
 
     for start in range(0, padded, 128):
         size = min(128, total - start)
@@ -191,43 +219,44 @@
                 value = jnp.concatenate([value, jnp.zeros((128 - size, units), F32)], axis=0)
             out_t[:, pl.ds(start, 128)] = value.T.astype(BF16)
 
-    part_copies = []
-    slots, share = part_buf.shape[1], part_buf.shape[3]
-    for step in range(steps):
+    def part_copy(step):
+        return pltpu.make_async_copy(part_buf.at[step], part_ref.at[step], part_sem.at[step])
+
+    def backward(step):
         for matrix, (left, right) in enumerate(((gate_t, tok_keep), (up_t, tok_keep), (hidden_t, scaled_keep))):
             part = matmul(left[...], right[step])
             part_buf[step, :, matrix] = part.reshape(slots, share, columns).astype(BF16)
-        part_copies.append(pltpu.make_async_copy(part_buf.at[step], part_ref.at[step], part_sem.at[step]))
-        part_copies[step].start()
-    for copy in part_copies:
-        copy.wait()
-
-
-def hidden_layer(got, weights, slots):
-    steps, _, units, columns = weights.shape
+        part_copy(step).start()
+
+    for step in range(steps):
+        backward(step)
+    for step in range(steps):
+        part_copy(step).wait()
+
+
+def hidden_layer(got, weights):
+    steps, slots, _, share, columns = weights.shape
+    units = slots * share
     rows = got.shape[0]
     total = rows // 16 * CAPACITY
     padded = -(-total // 128) * 128
-    width = steps * columns
-    far = pl.BlockSpec(memory_space=pltpu.MemorySpace.HBM)
-    near = pl.BlockSpec(memory_space=pltpu.VMEM)
-    part_shape = (steps, slots, 3, units // slots, columns)
+    quarter = steps * columns // 4
     return pl.pallas_call(
         hidden_kernel,
-        in_specs=[pl.BlockSpec(memory_space=pl.ANY), far],
-        out_specs=[far, near, near, near, near],
+        in_specs=[far(), far()],
+        out_specs=[far(), near(), near(), near(), near()],
         out_shape=[
-            jax.ShapeDtypeStruct(part_shape, BF16),
+            jax.ShapeDtypeStruct(weights.shape, BF16),
             jax.ShapeDtypeStruct((total, units), BF16),
             jax.ShapeDtypeStruct((total, units), BF16),
             jax.ShapeDtypeStruct((total, units), BF16),
             jax.ShapeDtypeStruct((steps, total, columns), BF16),
         ],
         scratch_shapes=[
-            pltpu.VMEM((steps, rows, columns), BF16),
-            pltpu.VMEM((rows, width // 4), BF16),
+            pltpu.VMEM((4, rows, quarter), BF16),
+            pltpu.VMEM((rows, quarter), BF16),
             pltpu.VMEM(weights.shape, BF16),
-            pltpu.VMEM(part_shape, BF16),
+            pltpu.VMEM(weights.shape, BF16),
             pltpu.VMEM((steps, padded, columns), BF16),
             pltpu.VMEM((steps, padded, columns), BF16),
             pltpu.VMEM((total, units), F32),
@@ -236,45 +265,54 @@
             pltpu.VMEM((units, padded), BF16),
             pltpu.VMEM((units, padded), BF16),
             pltpu.VMEM((units, padded), BF16),
-            pltpu.SemaphoreType.DMA((steps,)),
+            pltpu.SemaphoreType.DMA((4,)),
             pltpu.SemaphoreType.DMA,
-            pltpu.SemaphoreType.DMA((steps,)),
+            pltpu.SemaphoreType.DMA((4,)),
             pltpu.SemaphoreType.DMA((steps,)),
         ],
-        compiler_params=params(),
+        compiler_params=params(56),
     )(got, weights)
 
 
-def pair_kernel(gate_grad_ref, up_grad_ref, hidden_ref, scaled_ref, w_ref, out_ref, w_buf, w_sem):
-    steps, _, units, columns = w_buf.shape
+def pair_kernel(
+    gate_grad_ref, up_grad_ref, hidden_ref, scaled_ref, w_ref, out_ref, w_buf, rest_acc, dot_acc, w_sem
+):
+    steps, _, _, _, columns = w_buf.shape
     mains = out_ref.shape[0]
     count = mains // MAIN
     rests = count * 2
     width = steps * columns
     per_quarter = width // 4 // columns
-    copies = [pltpu.make_async_copy(w_ref.at[step], w_buf.at[step], w_sem.at[step]) for step in range(steps)]
-    for copy in copies:
-        copy.start()
-
+
+    def w_copy(step):
+        return pltpu.make_async_copy(w_ref.at[step], w_buf.at[step], w_sem.at[step])
+
+    for step in range(3):
+        w_copy(step).start()
+    rest_acc[...] = jnp.zeros_like(rest_acc)
+    dot_acc[...] = jnp.zeros_like(dot_acc)
     row, column = iota((mains, rests), 0), iota((mains, rests), 1)
     inner = row & 7
-    rest_sums = [None] * per_quarter
-    dots = None
-    for step in range(steps):
-        copies[step].wait()
-        grad = matmul(gate_grad_ref[...], w_buf[step, 0]) + matmul(up_grad_ref[...], w_buf[step, 1])
+    in_place = column == (row >> 3) * 2 + (inner & 1)
+
+    def one(step):
+        if step + 3 < steps:
+            w_copy(step + 3).start()
+        w_copy(step).wait()
+        grad = matmul(gate_grad_ref[...], whole(w_buf[step, :, 0]))
+        grad += matmul(up_grad_ref[...], whole(w_buf[step, :, 1]))
         grad = grad.astype(BF16)
         out_ref[:, pl.ds(step * columns, columns)] = grad[:mains]
-        placed = ones_where(((inner >> 1) == step // per_quarter) & (column == (row >> 3) * 2 + (inner & 1)))
-        moved = matmul(placed, grad[mains:])
-        which = step % per_quarter
-        rest_sums[which] = moved if rest_sums[which] is None else rest_sums[which] + moved
-        term = matmul(hidden_ref[...], w_buf[step, 2]) * scaled_ref[step].astype(F32)
-        dots = term if dots is None else dots + term
-
+        placed = ones_where(in_place & ((inner >> 1) == step // per_quarter))
+        rest_acc[step % per_quarter] += matmul(placed, grad[mains:])
+        dot_acc[...] += matmul(hidden_ref[...], whole(w_buf[step, :, 2])) * scaled_ref[step].astype(F32)
+
+    for step in range(steps):
+        one(step)
     for which in range(per_quarter):
-        out_ref[:, pl.ds(width + which * columns, columns)] = rest_sums[which].astype(BF16)
-    dots = jnp.broadcast_to(jnp.sum(dots, axis=1, keepdims=True), (mains + rests, LANES)).astype(BF16)
+        out_ref[:, pl.ds(width + which * columns, columns)] = rest_acc[which].astype(BF16)
+    dots = jnp.sum(dot_acc[...], axis=1, keepdims=True)
+    dots = jnp.broadcast_to(dots, (mains + rests, LANES)).astype(BF16)
     moved = matmul(ones_where((inner < 2) & (column == (row >> 3) * 2 + inner)), dots[mains:])
     lane = iota((mains, LANES), 1)
     out_ref[:, pl.ds(width + width // 4, LANES)] = jnp.where(
@@ -283,17 +321,22 @@
 
 
 def pair_layer(gate_grad, up_grad, hidden, scaled, weights):
-    steps, _, units, columns = weights.shape
-    mains = gate_grad.shape[0] // CAPACITY * MAIN
+    steps, _, _, _, columns = weights.shape
+    total = gate_grad.shape[0]
+    mains = total // CAPACITY * MAIN
     width = steps * columns
-    near = pl.BlockSpec(memory_space=pltpu.VMEM)
     return pl.pallas_call(
         pair_kernel,
-        in_specs=[near, near, near, near, pl.BlockSpec(memory_space=pltpu.MemorySpace.HBM)],
-        out_specs=near,
+        in_specs=[near(), near(), near(), near(), far()],
+        out_specs=near(),
         out_shape=jax.ShapeDtypeStruct((mains, width + width // 4 + LANES), BF16),
-        scratch_shapes=[pltpu.VMEM(weights.shape, BF16), pltpu.SemaphoreType.DMA((steps,))],
-        compiler_params=params(),
+        scratch_shapes=[
+            pltpu.VMEM(weights.shape, BF16),
+            pltpu.VMEM((width // 4 // columns, mains, columns), F32),
+            pltpu.VMEM((total, columns), F32),
+            pltpu.SemaphoreType.DMA((steps,)),
+        ],
+        compiler_params=params(56),
     )(gate_grad, up_grad, hidden, scaled, weights)
 
 
@@ -331,21 +374,21 @@
     code = jnp.where(inner < 2, (cell >> 3) * 16 + MAIN + inner, -1)
     found = []
     for main_hit, mine in ((main_first, code_first), (main_second, code_second)):
-        of_main = matmul(ones_where(main_hit), probs)[:, 0:1]
-        of_rest = matmul(ones_where(code == mine), probs)[:, LANES // 2 : LANES // 2 + 1]
+        of_main = matmul_tt(probs, ones_where(main_hit))[0:1, :]
+        of_rest = matmul_tt(probs, ones_where(code == mine))[LANES // 2 : LANES // 2 + 1, :]
         found.append(of_main + of_rest)
-    prob_ref[...] = (jnp.concatenate(found, axis=1) / weights_ref[...].astype(F32)).astype(BF16)
-
-
-def combine(routed_slots, route_probs, back, tokens, width):
+    prob_ref[...] = (jnp.concatenate(found, axis=0) / weights_ref[...].astype(F32)).astype(BF16)
+
+
+def combine(routed_slots, probs_t, back, tokens, width):
     return pl.pallas_call(
         combine_kernel,
         out_shape=[
             jax.ShapeDtypeStruct((tokens, width), BF16),
-            jax.ShapeDtypeStruct((tokens, 2), BF16),
+            jax.ShapeDtypeStruct((2, tokens), BF16),
         ],
         compiler_params=params(),
-    )(routed_slots, route_probs, back)
+    )(routed_slots, probs_t, back)
 
 
 def fold_kernel(placement_ref, part_ref, gate_ref, up_ref, down_ref, total):
@@ -389,25 +432,23 @@
     token_rows, width = tokens.shape
     columns = width // groups
     experts, share, _ = w_gate.shape
-    hidden = share * slots
-
-    index = jnp.concatenate([lax.axis_index("dp").astype(I32)[None], placement])
-    wanted = pick(index, w_gate, w_up, w_down, slots, columns)
+
+    wanted = pick(placement, w_gate, w_up, w_down, slots, columns)
     payload = pack(routed_slots.T, route_probs.T.astype(F32), tokens, cotangent, slots)
     mine = over_expert(wanted)
     mine, payload = lax.optimization_barrier((mine, payload))
-    mine = mine.transpose(1, 0, 2, 3).reshape(3, hidden, columns)
     weights = lax.all_gather(mine, "dp", axis=0)
     got = over_expert(payload.reshape(slots, 2 * MAIN, -1)).reshape(payload.shape)
 
-    parts, gate_grad, up_grad, hidden_rows, scaled = hidden_layer(got, weights, slots)
+    parts, gate_grad, up_grad, hidden_rows, scaled = hidden_layer(got, weights)
     summed = lax.psum_scatter(parts, "dp", scatter_dimension=0)
     pairs = pair_layer(gate_grad, up_grad, hidden_rows, scaled, weights)
     back = over_expert(pairs.reshape(slots, MAIN, -1)).reshape(pairs.shape)
-    token_grad, prob_grad = combine(routed_slots, route_probs, back, token_rows, width)
-
+    token_grad, prob_grad = combine(routed_slots, route_probs.T, back, token_rows, width)
+
+    summed, token_grad, prob_grad = lax.optimization_barrier((summed, token_grad, prob_grad))
     grads = fold(placement, over_expert(summed), experts)
-    return (token_grad, prob_grad, *grads)
+    return (token_grad, prob_grad.T, *grads)
 
 
 def solution(mesh):

time: 249 us -> 243 us (0.976)
  local copies, waits for them, and re-layouts: 5.69 us -> 1.17 us
    all_to_all x2, waiting for transfers between devices: 53.4 us -> 56.7 us  [over_expert(): lax.all_to_all(value, 'expert', split_axis=0, concat_axis=0, tiled=True)]
where the time goes in v3:
time: 243 us; the launch traced here: 242 us
  blocking collectives  109 us (45%)
  waiting for transfers between devices  62.8 us (26%)
  Pallas kernels  34.8 us (14%)
  starting transfers between devices  20.3 us (8%)
  between operations  14.2 us (6%)
    all_to_all x2, blocking collectives, over_expert(): lax.all_to_all(value, 'expert', split_axis=0, concat_axis=0, tiled=True)  109 us
    all_to_all x2, waiting for transfers between devices, over_expert(): lax.all_to_all(value, 'expert', split_axis=0, concat_axis=0, tiled=True)  56.7 us
    all_to_all x2, starting transfers between devices, over_expert(): lax.all_to_all(value, 'expert', split_axis=0, concat_axis=0, tiled=True)  20.2 us
    pallas_call x1, Pallas kernels, hidden_layer(): pl.pallas_call(hidden_kernel, in_specs=[far(), far()], out_specs=[far(),...  15.3 us
    pallas_call x1, Pallas kernels, pair_layer(): pl.pallas_call(pair_kernel, in_specs=[near(), near(), near(), near(), far...  11.1 us
    reduce_scatter x1, waiting for transfers between devices, on_device(): summed = lax.psum_scatter(parts, 'dp', scatter_dimension=0)  6.08 us
  transfers between devices with their start and end apart: 4, of which 3 were waited for; matrix products, arithmetic and copies ran while one was open for 0% of the time, Pallas kernels for 6%

profile of v3, /device:TPU:9, one launch (start us, length us, event | category | flops | bytes accessed | tf_op | source)
XLA Modules:
  0.0 242.2 jit_solution(12359758926489913005)
XLA Ops:
  7.2 2.9 %shard_map.119 = bf16[32,3,24,256]{3,2,1,0:T(8,128)(2,1)} custom-call(s32[32]{0:T(128)} %placement_ref.3, bf16[16,24,2048]{2,1,0:T(8,128)(2,1)} %gate_ref.1, bf16[16,24,2048]{2,1,0:T(8,128)(2,1)} %up_ref.1, bf16[16,24,2048]{2,1,0:T(8,128)(2,1)} %down_ref.1), custom_call_target="tpu_custom_call" | custom-call | tf_op jit(solution)/shard_map/pallas_call | solution.py:67
  10.1 0.0 copy-start.4
  10.1 0.0 copy-start
  10.1 0.0 copy-start.2
  10.1 11.3 %all-to-all-start = ((bf16[32,3,24,256]{3,2,1,0:T(8,128)(2,1)}), bf16[32,3,24,256]{3,2,1,0:T(8,128)(2,1)}, u32[]{:S(2)}, u32[]{:S(2)}) async-start(bf16[32,3,24,256]{3,2,1,0:T(8,128)(2,1)} %shard_map.119), calls=%async_computation | async-start | bytes 2359296 | tf_op jit(solution)/shard_map/all_to_all | solution.py:426
  21.4 0.0 all-gather.3.cloned.1.call-start
  21.4 0.0 copy-done.4
  21.5 0.0 copy-done
  21.5 0.0 copy-done.2
  21.5 0.0 copy-start.1
  21.5 1.0 copy-done.1
  22.5 2.1 shard_map.120
  24.6 24.3 %all-to-all-done = bf16[32,3,24,256]{3,2,1,0:T(8,128)(2,1)} async-done(((bf16[32,3,24,256]{3,2,1,0:T(8,128)(2,1)}), bf16[32,3,24,256]{3,2,1,0:T(8,128)(2,1)}, u32[]{:S(2)}, u32[]{:S(2)}) %all-to-all-start) | async-done | bytes 1179680 | tf_op jit(solution)/shard_map/all_to_all | solution.py:426
  48.9 0.0 all-gather.3.cloned.1.call-update
  48.9 0.0 reduce-scatter.2.cloned.1.call-start
  49.0 66.7 %all_to_all.20 = bf16[32,16,2560]{2,1,0:T(8,128)(2,1)} all-to-all(bf16[32,16,2560]{2,1,0:T(8,128)(2,1)S(1)} %bitcast.10), channel_id=1, replica_groups=mesh['dp'=8,'expert'=32] {'expert'}, dimensions={0} | all-to-all | bytes 5242880 | tf_op jit(solution)/shard_map/all_to_all | solution.py:426
  115.7 0.0 all-gather.3.cloned.1.call-done
  115.7 15.3 %shard_map.121 = (bf16[8,32,3,24,256]{4,3,2,1,0:T(8,128)(2,1)}, bf16[320,768]{1,0:T(8,128)(2,1)}, bf16[320,768]{1,0:T(8,128)(2,1)}, bf16[320,768]{1,0:T(8,128)(2,1)}, bf16[8,320,256]{2,1,0:T(8,128)(2,1)}) custom-call(bf16[512,2560]{1,0:T(8,128)(2,1)} %bitcast.16, bf16[8,32,3,24,256]{4,3,2,1,0:T(8,128)(2,1)} %bitcast.14), custom_call_target="tpu_custom_call" | custom-call | tf_op jit(solution)/shard_map/pallas_call | solution.py:244
  131.0 0.0 reduce-scatter.2.cloned.1.call-update
  131.1 11.1 %shard_map.122 = bf16[256,2688]{1,0:T(8,128)(2,1)} custom-call(bf16[320,768]{1,0:T(8,128)(2,1)} %get-tuple-element.23.gate_grad_ref, bf16[320,768]{1,0:T(8,128)(2,1)} %get-tuple-element.24.up_grad_ref, bf16[320,768]{1,0:T(8,128)(2,1)} %get-tuple-element.25.hidden_ref, bf16[8,320,256]{2,1,0:T(8,128)(2,1)} %get-tuple-element.26.scaled_ref, ...), custom_call_target="tpu_custom_call" | custom-call | tf_op jit(solution)/shard_map/pallas_call | solution.py:328
  142.2 8.9 %all-to-all-start.2 = ((bf16[32,8,2688]{2,1,0:T(8,128)(2,1)}), bf16[32,8,2688]{2,1,0:T(8,128)(2,1)S(1)}, u32[]{:S(2)}, u32[]{:S(2)}) async-start(bf16[32,8,2688]{2,1,0:T(8,128)(2,1)} %bitcast.17), calls=%async_computation.3 | async-start | bytes 2752512 | tf_op jit(solution)/shard_map/all_to_all | solution.py:426
  151.0 0.1 copy.14.slots_ref
  151.2 32.4 %all-to-all-done.2 = bf16[32,8,2688]{2,1,0:T(8,128)(2,1)S(1)} async-done(((bf16[32,8,2688]{2,1,0:T(8,128)(2,1)}), bf16[32,8,2688]{2,1,0:T(8,128)(2,1)S(1)}, u32[]{:S(2)}, u32[]{:S(2)}) %all-to-all-start.2) | async-done | bytes 1376288 | tf_op jit(solution)/shard_map/all_to_all | solution.py:426
  183.5 0.0 copy-start.3
  183.5 1.6 shard_map.123
  185.2 6.1 %reduce-scatter.2.cloned.1.call-done = bf16[1,32,3,24,256]{4,3,2,1,0:T(8,128)(2,1)} async-done(((bf16[8,32,3,24,256]{4,3,2,1,0:T(8,128)(2,1)}), bf16[1,32,3,24,256]{4,3,2,1,0:T(8,128)(2,1)}) %reduce-scatter.2.cloned.1.call-update) | async-done | bytes 1179664 | tf_op jit(solution)/shard_map/reduce_scatter | solution.py:444
  191.3 42.2 %all_to_all.21.part_ref = bf16[32,3,24,256]{3,2,1,0:T(8,128)(2,1)S(1)} all-to-all(bf16[32,3,24,256]{3,2,1,0:T(8,128)(2,1)} %bitcast.18), channel_id=1, replica_groups=mesh['dp'=8,'expert'=32] {'expert'}, dimensions={0} | all-to-all | bytes 2359296 | tf_op jit(solution)/shard_map/all_to_all | solution.py:426
  233.5 0.0 copy-done.3
  233.5 1.8 shard_map.124
  (1 shorter events, 0.0 us)
Async XLA Ops:
  10.1 11.4 %copy-start.4 = (bf16[128,2]{0,1:T(2,128)(2,1)S(1)}, bf16[128,2]{0,1:T(2,128)(2,1)}, u32[]{:S(2)}) copy-start(bf16[128,2]{0,1:T(2,128)(2,1)} %param.11) | copy-start | bytes 1540
  10.1 11.4 %copy-start = (bf16[128,2048]{1,0:T(8,128)(2,1)S(1)}, bf16[128,2048]{1,0:T(8,128)(2,1)}, u32[]{:S(2)}) copy-start(bf16[128,2048]{1,0:T(8,128)(2,1)} %tok_ref.1) | copy-start | bytes 1572868
  10.1 11.4 %copy-start.2 = (s32[128,2]{0,1:T(2,128)S(1)}, s32[128,2]{0,1:T(2,128)}, u32[]{:S(2)}) copy-start(s32[128,2]{0,1:T(2,128)} %param.10) | copy-start | bytes 3076
  10.1 38.8 %all-to-all-start = ((bf16[32,3,24,256]{3,2,1,0:T(8,128)(2,1)}), bf16[32,3,24,256]{3,2,1,0:T(8,128)(2,1)}, u32[]{:S(2)}, u32[]{:S(2)}) async-start(bf16[32,3,24,256]{3,2,1,0:T(8,128)(2,1)} %shard_map.119), calls=%async_computation | async-start | bytes 2359296 | tf_op jit(solution)/shard_map/all_to_all | solution.py:426
  21.4 94.3 %all-gather.3.cloned.1.call-start = ((), (), s32[]{:S(2)}) async-start(), calls=%async_computation.6 | async-start | bytes 10616832 | tf_op jit(solution)/shard_map/all_gather | solution.py:440
  21.5 1.0 copy-start.1
  48.9 142.3 %reduce-scatter.2.cloned.1.call-start = ((), (), s32[]{:S(2)}) async-start(), calls=%async_computation.5 | async-start | bytes 10616832 | tf_op jit(solution)/shard_map/reduce_scatter | solution.py:444
  142.2 41.4 %all-to-all-start.2 = ((bf16[32,8,2688]{2,1,0:T(8,128)(2,1)}), bf16[32,8,2688]{2,1,0:T(8,128)(2,1)S(1)}, u32[]{:S(2)}, u32[]{:S(2)}) async-start(bf16[32,8,2688]{2,1,0:T(8,128)(2,1)} %bitcast.17), calls=%async_computation.3 | async-start | bytes 2752512 | tf_op jit(solution)/shard_map/all_to_all | solution.py:426
  183.5 50.0 %copy-start.3 = (s32[32]{0:T(128)S(1)}, s32[32]{0:T(128)}, u32[]{:S(2)}) copy-start(s32[32]{0:T(128)} %placement_ref.3) | copy-start | bytes 388
Sparse Core Ops, SparseCore 0:
  49.1 57.1 all-gather.2
  131.2 60.0 reduce-scatter.1

commit v4 on v3

--- a/solution.py
+++ b/solution.py
@@ -140,7 +140,7 @@
     got_ref, w_ref,
     part_ref, gate_grad_ref, up_grad_ref, hidden_ref, scaled_ref,
     got_buf, rest_buf, w_buf, part_buf, tok_keep, scaled_keep, gate_acc, up_acc, down_acc, gate_t, up_t, hidden_t,
-    got_sem, rest_sem, w_sem, part_sem,
+    grad_keep, scaled_out, got_sem, rest_sem, w_sem, part_sem, grad_sem, scaled_sem,
 ):
     quarters, rows, quarter = got_buf.shape
     steps, slots, _, share, columns = w_buf.shape
@@ -158,6 +158,10 @@
     def w_copy(part):
         at = pl.ds(part * each, each)
         return pltpu.make_async_copy(w_ref.at[at], w_buf.at[at], w_sem.at[part])
+
+    def scaled_copy(part):
+        at = pl.ds(part * each, each)
+        return pltpu.make_async_copy(scaled_out.at[at], scaled_ref.at[at], scaled_sem.at[part])
 
     rest_copy = pltpu.make_async_copy(got_ref.at[:, pl.ds(quarters * quarter, quarter)], rest_buf, rest_sem)
     rest_copy.start()
@@ -191,7 +195,8 @@
             at = slice(i * columns, (i + 1) * columns)
             tok_keep[part * each + i, 0:total] = tok[:, at]
             scaled_keep[part * each + i, 0:total] = scaled[:, at]
-            scaled_ref[part * each + i] = scaled[:, at]
+            scaled_out[part * each + i] = scaled[:, at]
+        scaled_copy(part).start()
         w_copy(part).wait()
         for acc, left, matrix in ((gate_acc, tok, 0), (up_acc, tok, 1), (down_acc, scaled, 2)):
             right = jnp.concatenate([whole(w_buf[part * each + i, :, matrix]) for i in range(each)], axis=1)
@@ -209,15 +214,18 @@
         hidden = swish * up_pre
         gate_grad = hidden_grad * up_pre * sigma * (1.0 + gate_pre * (1.0 - sigma))
         up_grad = hidden_grad * swish
-        for value, out, out_t in (
-            (hidden, hidden_ref, hidden_t),
-            (gate_grad, gate_grad_ref, gate_t),
-            (up_grad, up_grad_ref, up_t),
-        ):
-            out[at, :] = value.astype(BF16)
+        for which, (value, out_t) in enumerate(((gate_grad, gate_t), (up_grad, up_t), (hidden, hidden_t))):
+            grad_keep[which, at, :] = value.astype(BF16)
             if size < 128:
                 value = jnp.concatenate([value, jnp.zeros((128 - size, units), F32)], axis=0)
             out_t[:, pl.ds(start, 128)] = value.T.astype(BF16)
+
+    grad_copies = [
+        pltpu.make_async_copy(grad_keep.at[which], out, grad_sem.at[which])
+        for which, out in enumerate((gate_grad_ref, up_grad_ref, hidden_ref))
+    ]
+    for copy in grad_copies:
+        copy.start()
 
     def part_copy(step):
         return pltpu.make_async_copy(part_buf.at[step], part_ref.at[step], part_sem.at[step])
@@ -230,6 +238,10 @@
 
     for step in range(steps):
         backward(step)
+    for part in range(quarters):
+        scaled_copy(part).wait()
+    for copy in grad_copies:
+        copy.wait()
     for step in range(steps):
         part_copy(step).wait()
 
@@ -244,7 +256,7 @@
     return pl.pallas_call(
         hidden_kernel,
         in_specs=[far(), far()],
-        out_specs=[far(), near(), near(), near(), near()],
+        out_specs=[far()] * 5,
         out_shape=[
             jax.ShapeDtypeStruct(weights.shape, BF16),
             jax.ShapeDtypeStruct((total, units), BF16),
@@ -265,10 +277,14 @@
             pltpu.VMEM((units, padded), BF16),
             pltpu.VMEM((units, padded), BF16),
             pltpu.VMEM((units, padded), BF16),
+            pltpu.VMEM((3, total, units), BF16),
+            pltpu.VMEM((steps, total, columns), BF16),
             pltpu.SemaphoreType.DMA((4,)),
             pltpu.SemaphoreType.DMA,
             pltpu.SemaphoreType.DMA((4,)),
             pltpu.SemaphoreType.DMA((steps,)),
+            pltpu.SemaphoreType.DMA((3,)),
+            pltpu.SemaphoreType.DMA((4,)),
         ],
         compiler_params=params(56),
     )(got, weights)

time: 243 us -> 241 us (level)
  no operation moved by 1% of the time
where the time goes in v4:
time: 241 us
  blocking collectives  109 us (45%)
  waiting for transfers between devices  62.8 us (26%)
  Pallas kernels  33.3 us (14%)
  starting transfers between devices  20.3 us (8%)
  between operations  14.2 us (6%)
    all_to_all x2, blocking collectives, over_expert(): lax.all_to_all(value, 'expert', split_axis=0, concat_axis=0, tiled=True)  109 us
    all_to_all x2, waiting for transfers between devices, over_expert(): lax.all_to_all(value, 'expert', split_axis=0, concat_axis=0, tiled=True)  56.7 us
    all_to_all x2, starting transfers between devices, over_expert(): lax.all_to_all(value, 'expert', split_axis=0, concat_axis=0, tiled=True)  20.2 us
    pallas_call x1, Pallas kernels, hidden_layer(): pl.pallas_call(hidden_kernel, in_specs=[far(), far()], out_specs=[far()]...  13.8 us
    pallas_call x1, Pallas kernels, pair_layer(): pl.pallas_call(pair_kernel, in_specs=[near(), near(), near(), near(), far...  11.1 us
    reduce_scatter x1, waiting for transfers between devices, on_device(): summed = lax.psum_scatter(parts, 'dp', scatter_dimension=0)  6.06 us
  transfers between devices with their start and end apart: 4, of which 3 were waited for; matrix products, arithmetic and copies ran while one was open for 0% of the time, Pallas kernels for 6%

profile of v4, /device:TPU:9, one launch (start us, length us, event | category | flops | bytes accessed | tf_op | source)
XLA Modules:
  0.0 240.6 jit_solution(2112615513710011006)
XLA Ops:
  7.2 2.9 %shard_map.119 = bf16[32,3,24,256]{3,2,1,0:T(8,128)(2,1)} custom-call(s32[32]{0:T(128)} %placement_ref.3, bf16[16,24,2048]{2,1,0:T(8,128)(2,1)} %gate_ref.1, bf16[16,24,2048]{2,1,0:T(8,128)(2,1)} %up_ref.1, bf16[16,24,2048]{2,1,0:T(8,128)(2,1)} %down_ref.1), custom_call_target="tpu_custom_call" | custom-call | tf_op jit(solution)/shard_map/pallas_call | solution.py:67
  10.1 0.0 copy-start.4
  10.1 0.0 copy-start
  10.1 0.0 copy-start.2
  10.1 11.3 %all-to-all-start = ((bf16[32,3,24,256]{3,2,1,0:T(8,128)(2,1)}), bf16[32,3,24,256]{3,2,1,0:T(8,128)(2,1)}, u32[]{:S(2)}, u32[]{:S(2)}) async-start(bf16[32,3,24,256]{3,2,1,0:T(8,128)(2,1)} %shard_map.119), calls=%async_computation | async-start | bytes 2359296 | tf_op jit(solution)/shard_map/all_to_all | solution.py:442
  21.4 0.0 all-gather.3.cloned.1.call-start
  21.4 0.0 copy-done.4
  21.5 0.0 copy-done
  21.5 0.0 copy-done.2
  21.5 0.0 copy-start.1
  21.5 1.0 copy-done.1
  22.5 2.1 shard_map.120
  24.6 24.3 %all-to-all-done = bf16[32,3,24,256]{3,2,1,0:T(8,128)(2,1)} async-done(((bf16[32,3,24,256]{3,2,1,0:T(8,128)(2,1)}), bf16[32,3,24,256]{3,2,1,0:T(8,128)(2,1)}, u32[]{:S(2)}, u32[]{:S(2)}) %all-to-all-start) | async-done | bytes 1179680 | tf_op jit(solution)/shard_map/all_to_all | solution.py:442
  48.9 0.0 all-gather.3.cloned.1.call-update
  48.9 0.0 reduce-scatter.2.cloned.1.call-start
  49.0 66.7 %all_to_all.20 = bf16[32,16,2560]{2,1,0:T(8,128)(2,1)} all-to-all(bf16[32,16,2560]{2,1,0:T(8,128)(2,1)S(1)} %bitcast.10), channel_id=1, replica_groups=mesh['dp'=8,'expert'=32] {'expert'}, dimensions={0} | all-to-all | bytes 5242880 | tf_op jit(solution)/shard_map/all_to_all | solution.py:442
  115.7 0.0 all-gather.3.cloned.1.call-done
  115.7 13.8 %shard_map.121 = (bf16[8,32,3,24,256]{4,3,2,1,0:T(8,128)(2,1)}, bf16[320,768]{1,0:T(8,128)(2,1)}, bf16[320,768]{1,0:T(8,128)(2,1)}, bf16[320,768]{1,0:T(8,128)(2,1)}, bf16[8,320,256]{2,1,0:T(8,128)(2,1)}) custom-call(bf16[512,2560]{1,0:T(8,128)(2,1)} %bitcast.16, bf16[8,32,3,24,256]{4,3,2,1,0:T(8,128)(2,1)} %bitcast.14), custom_call_target="tpu_custom_call" | custom-call | tf_op jit(solution)/shard_map/pallas_call | solution.py:256
  129.5 0.0 reduce-scatter.2.cloned.1.call-update
  129.5 11.1 %shard_map.122 = bf16[256,2688]{1,0:T(8,128)(2,1)} custom-call(bf16[320,768]{1,0:T(8,128)(2,1)} %get-tuple-element.23.gate_grad_ref, bf16[320,768]{1,0:T(8,128)(2,1)} %get-tuple-element.24.up_grad_ref, bf16[320,768]{1,0:T(8,128)(2,1)} %get-tuple-element.25.hidden_ref, bf16[8,320,256]{2,1,0:T(8,128)(2,1)} %get-tuple-element.26.scaled_ref, ...), custom_call_target="tpu_custom_call" | custom-call | tf_op jit(solution)/shard_map/pallas_call | solution.py:344
  140.6 8.9 %all-to-all-start.2 = ((bf16[32,8,2688]{2,1,0:T(8,128)(2,1)}), bf16[32,8,2688]{2,1,0:T(8,128)(2,1)S(1)}, u32[]{:S(2)}, u32[]{:S(2)}) async-start(bf16[32,8,2688]{2,1,0:T(8,128)(2,1)} %bitcast.17), calls=%async_computation.3 | async-start | bytes 2752512 | tf_op jit(solution)/shard_map/all_to_all | solution.py:442
  149.5 0.1 copy.14.slots_ref
  149.6 32.4 %all-to-all-done.2 = bf16[32,8,2688]{2,1,0:T(8,128)(2,1)S(1)} async-done(((bf16[32,8,2688]{2,1,0:T(8,128)(2,1)}), bf16[32,8,2688]{2,1,0:T(8,128)(2,1)S(1)}, u32[]{:S(2)}, u32[]{:S(2)}) %all-to-all-start.2) | async-done | bytes 1376288 | tf_op jit(solution)/shard_map/all_to_all | solution.py:442
  182.0 0.0 copy-start.3
  182.0 1.6 shard_map.123
  183.7 6.1 %reduce-scatter.2.cloned.1.call-done = bf16[1,32,3,24,256]{4,3,2,1,0:T(8,128)(2,1)} async-done(((bf16[8,32,3,24,256]{4,3,2,1,0:T(8,128)(2,1)}), bf16[1,32,3,24,256]{4,3,2,1,0:T(8,128)(2,1)}) %reduce-scatter.2.cloned.1.call-update) | async-done | bytes 1179664 | tf_op jit(solution)/shard_map/reduce_scatter | solution.py:460
  189.7 42.2 %all_to_all.21.part_ref = bf16[32,3,24,256]{3,2,1,0:T(8,128)(2,1)S(1)} all-to-all(bf16[32,3,24,256]{3,2,1,0:T(8,128)(2,1)} %bitcast.18), channel_id=1, replica_groups=mesh['dp'=8,'expert'=32] {'expert'}, dimensions={0} | all-to-all | bytes 2359296 | tf_op jit(solution)/shard_map/all_to_all | solution.py:442
  232.0 0.0 copy-done.3
  232.0 1.8 shard_map.124
  (1 shorter events, 0.0 us)
Async XLA Ops:
  10.1 11.4 %copy-start.4 = (bf16[128,2]{0,1:T(2,128)(2,1)S(1)}, bf16[128,2]{0,1:T(2,128)(2,1)}, u32[]{:S(2)}) copy-start(bf16[128,2]{0,1:T(2,128)(2,1)} %param.11) | copy-start | bytes 1540
  10.1 11.4 %copy-start = (bf16[128,2048]{1,0:T(8,128)(2,1)S(1)}, bf16[128,2048]{1,0:T(8,128)(2,1)}, u32[]{:S(2)}) copy-start(bf16[128,2048]{1,0:T(8,128)(2,1)} %tok_ref.1) | copy-start | bytes 1572868
  10.1 11.4 %copy-start.2 = (s32[128,2]{0,1:T(2,128)S(1)}, s32[128,2]{0,1:T(2,128)}, u32[]{:S(2)}) copy-start(s32[128,2]{0,1:T(2,128)} %param.10) | copy-start | bytes 3076
  10.1 38.8 %all-to-all-start = ((bf16[32,3,24,256]{3,2,1,0:T(8,128)(2,1)}), bf16[32,3,24,256]{3,2,1,0:T(8,128)(2,1)}, u32[]{:S(2)}, u32[]{:S(2)}) async-start(bf16[32,3,24,256]{3,2,1,0:T(8,128)(2,1)} %shard_map.119), calls=%async_computation | async-start | bytes 2359296 | tf_op jit(solution)/shard_map/all_to_all | solution.py:442
  21.4 94.3 %all-gather.3.cloned.1.call-start = ((), (), s32[]{:S(2)}) async-start(), calls=%async_computation.6 | async-start | bytes 10616832 | tf_op jit(solution)/shard_map/all_gather | solution.py:456
  21.5 1.0 copy-start.1
  48.9 140.8 %reduce-scatter.2.cloned.1.call-start = ((), (), s32[]{:S(2)}) async-start(), calls=%async_computation.5 | async-start | bytes 10616832 | tf_op jit(solution)/shard_map/reduce_scatter | solution.py:460
  140.6 41.4 %all-to-all-start.2 = ((bf16[32,8,2688]{2,1,0:T(8,128)(2,1)}), bf16[32,8,2688]{2,1,0:T(8,128)(2,1)S(1)}, u32[]{:S(2)}, u32[]{:S(2)}) async-start(bf16[32,8,2688]{2,1,0:T(8,128)(2,1)} %bitcast.17), calls=%async_computation.3 | async-start | bytes 2752512 | tf_op jit(solution)/shard_map/all_to_all | solution.py:442
  182.0 49.9 %copy-start.3 = (s32[32]{0:T(128)S(1)}, s32[32]{0:T(128)}, u32[]{:S(2)}) copy-start(s32[32]{0:T(128)} %placement_ref.3) | copy-start | bytes 388
Sparse Core Ops, SparseCore 0:
  49.1 57.1 all-gather.2
  129.7 60.0 reduce-scatter.1

commit v5 on v4

--- a/solution.py
+++ b/solution.py
@@ -47,7 +47,7 @@
     return lax.dot_general(a, b, (((0,), (1,)), ((), ())), preferred_element_type=F32)
 
 
-def pick_kernel(placement_ref, gate_ref, up_ref, down_ref, out_ref, buf, sem):
+def pick_kernel(placement_ref, gate_ref, up_ref, down_ref, out_ref, buf, picked, sem, out_sem):
     columns = out_ref.shape[3]
     at = pl.ds(pl.multiple_of(lax.axis_index("dp") * columns, columns), columns)
     copies = [
@@ -56,10 +56,17 @@
     ]
     for copy in copies:
         copy.start()
+
+    def leave(matrix):
+        return pltpu.make_async_copy(picked.at[matrix], out_ref.at[:, matrix], out_sem.at[matrix])
+
     for matrix, copy in enumerate(copies):
         copy.wait()
         for slot in range(out_ref.shape[0]):
-            out_ref[slot, matrix] = buf[matrix, placement_ref[slot]]
+            picked[matrix, slot] = buf[matrix, placement_ref[slot]]
+        leave(matrix).start()
+    for matrix in range(3):
+        leave(matrix).wait()
 
 
 def pick(placement, w_gate, w_up, w_down, slots, columns):
@@ -67,9 +74,14 @@
     return pl.pallas_call(
         pick_kernel,
         in_specs=[pl.BlockSpec(memory_space=pltpu.SMEM), far(), far(), far()],
-        out_specs=near(),
+        out_specs=far(),
         out_shape=jax.ShapeDtypeStruct((slots, 3, share, columns), BF16),
-        scratch_shapes=[pltpu.VMEM((3, experts, share, columns), BF16), pltpu.SemaphoreType.DMA((3,))],
+        scratch_shapes=[
+            pltpu.VMEM((3, experts, share, columns), BF16),
+            pltpu.VMEM((3, slots, share, columns), BF16),
+            pltpu.SemaphoreType.DMA((3,)),
+            pltpu.SemaphoreType.DMA((3,)),
+        ],
         compiler_params=params(56),
     )(placement, w_gate, w_up, w_down)
 
@@ -139,7 +151,7 @@
 def hidden_kernel(
     got_ref, w_ref,
     part_ref, gate_grad_ref, up_grad_ref, hidden_ref, scaled_ref,
-    got_buf, rest_buf, w_buf, part_buf, tok_keep, scaled_keep, gate_acc, up_acc, down_acc, gate_t, up_t, hidden_t,
+    got_buf, rest_buf, w_buf, part_buf, tok_keep, scaled_keep, gate_acc, up_acc, down_acc, both_t, hidden_t,
     grad_keep, scaled_out, got_sem, rest_sem, w_sem, part_sem, grad_sem, scaled_sem,
 ):
     quarters, rows, quarter = got_buf.shape
@@ -205,6 +217,7 @@
 
     lax.fori_loop(0, quarters, forward, 0)
 
+    gate_t, up_t = both_t.at[0:units], both_t.at[units : 2 * units]
     for start in range(0, padded, 128):
         size = min(128, total - start)
         at = pl.ds(start, size)
@@ -231,9 +244,11 @@
         return pltpu.make_async_copy(part_buf.at[step], part_ref.at[step], part_sem.at[step])
 
     def backward(step):
-        for matrix, (left, right) in enumerate(((gate_t, tok_keep), (up_t, tok_keep), (hidden_t, scaled_keep))):
-            part = matmul(left[...], right[step])
-            part_buf[step, :, matrix] = part.reshape(slots, share, columns).astype(BF16)
+        both = matmul(both_t[...], tok_keep[step]).reshape(2, slots, share, columns).astype(BF16)
+        part_buf[step, :, 0] = both[0]
+        part_buf[step, :, 1] = both[1]
+        part = matmul(hidden_t[...], scaled_keep[step])
+        part_buf[step, :, 2] = part.reshape(slots, share, columns).astype(BF16)
         part_copy(step).start()
 
     for step in range(steps):
@@ -274,8 +289,7 @@
             pltpu.VMEM((total, units), F32),
             pltpu.VMEM((total, units), F32),
             pltpu.VMEM((total, units), F32),
-            pltpu.VMEM((units, padded), BF16),
-            pltpu.VMEM((units, padded), BF16),
+            pltpu.VMEM((2 * units, padded), BF16),
             pltpu.VMEM((units, padded), BF16),
             pltpu.VMEM((3, total, units), BF16),
             pltpu.VMEM((steps, total, columns), BF16),

time: 241 us -> 241 us (level)
  no operation moved by 1% of the time
where the time goes in v5:
time: 241 us; the launch traced here: 240 us
  blocking collectives  109 us (45%)
  waiting for transfers between devices  62.8 us (26%)
  Pallas kernels  33 us (14%)
  starting transfers between devices  20.3 us (8%)
  between operations  14.2 us (6%)
    all_to_all x2, blocking collectives, over_expert(): lax.all_to_all(value, 'expert', split_axis=0, concat_axis=0, tiled=True)  109 us
    all_to_all x2, waiting for transfers between devices, over_expert(): lax.all_to_all(value, 'expert', split_axis=0, concat_axis=0, tiled=True)  56.7 us
    all_to_all x2, starting transfers between devices, over_expert(): lax.all_to_all(value, 'expert', split_axis=0, concat_axis=0, tiled=True)  20.2 us
    pallas_call x1, Pallas kernels, hidden_layer(): pl.pallas_call(hidden_kernel, in_specs=[far(), far()], out_specs=[far()]...  13.7 us
    pallas_call x1, Pallas kernels, pair_layer(): pl.pallas_call(pair_kernel, in_specs=[near(), near(), near(), near(), far...  11.1 us
    reduce_scatter x1, waiting for transfers between devices, on_device(): summed = lax.psum_scatter(parts, 'dp', scatter_dimension=0)  6.09 us
  transfers between devices with their start and end apart: 4, of which 3 were waited for; matrix products, arithmetic and copies ran while one was open for 0% of the time, Pallas kernels for 6%

profile of v5, /device:TPU:9, one launch (start us, length us, event | category | flops | bytes accessed | tf_op | source)
XLA Modules:
  0.0 240.4 jit_solution(10127435104851851756)
XLA Ops:
  7.2 2.8 %shard_map.119 = bf16[32,3,24,256]{3,2,1,0:T(8,128)(2,1)} custom-call(s32[32]{0:T(128)} %placement_ref.3, bf16[16,24,2048]{2,1,0:T(8,128)(2,1)} %gate_ref.1, bf16[16,24,2048]{2,1,0:T(8,128)(2,1)} %up_ref.1, bf16[16,24,2048]{2,1,0:T(8,128)(2,1)} %down_ref.1), custom_call_target="tpu_custom_call" | custom-call | tf_op jit(solution)/shard_map/pallas_call | solution.py:74
  9.9 0.0 copy-start.4
  9.9 0.0 copy-start
  10.0 0.0 copy-start.2
  10.0 11.3 %all-to-all-start = ((bf16[32,3,24,256]{3,2,1,0:T(8,128)(2,1)}), bf16[32,3,24,256]{3,2,1,0:T(8,128)(2,1)}, u32[]{:S(2)}, u32[]{:S(2)}) async-start(bf16[32,3,24,256]{3,2,1,0:T(8,128)(2,1)} %shard_map.119), calls=%async_computation | async-start | bytes 2359296 | tf_op jit(solution)/shard_map/all_to_all | solution.py:456
  21.3 0.0 all-gather.3.cloned.1.call-start
  21.3 0.0 copy-done.4
  21.3 0.0 copy-done
  21.3 0.0 copy-done.2
  21.4 0.0 copy-start.1
  21.4 1.0 copy-done.1
  22.4 2.1 shard_map.120
  24.5 24.3 %all-to-all-done = bf16[32,3,24,256]{3,2,1,0:T(8,128)(2,1)} async-done(((bf16[32,3,24,256]{3,2,1,0:T(8,128)(2,1)}), bf16[32,3,24,256]{3,2,1,0:T(8,128)(2,1)}, u32[]{:S(2)}, u32[]{:S(2)}) %all-to-all-start) | async-done | bytes 1179680 | tf_op jit(solution)/shard_map/all_to_all | solution.py:456
  48.8 0.0 all-gather.3.cloned.1.call-update
  48.8 0.0 reduce-scatter.2.cloned.1.call-start
  48.9 66.7 %all_to_all.20 = bf16[32,16,2560]{2,1,0:T(8,128)(2,1)} all-to-all(bf16[32,16,2560]{2,1,0:T(8,128)(2,1)S(1)} %bitcast.10), channel_id=1, replica_groups=mesh['dp'=8,'expert'=32] {'expert'}, dimensions={0} | all-to-all | bytes 5242880 | tf_op jit(solution)/shard_map/all_to_all | solution.py:456
  115.6 0.0 all-gather.3.cloned.1.call-done
  115.6 13.7 %shard_map.121 = (bf16[8,32,3,24,256]{4,3,2,1,0:T(8,128)(2,1)}, bf16[320,768]{1,0:T(8,128)(2,1)}, bf16[320,768]{1,0:T(8,128)(2,1)}, bf16[320,768]{1,0:T(8,128)(2,1)}, bf16[8,320,256]{2,1,0:T(8,128)(2,1)}) custom-call(bf16[512,2560]{1,0:T(8,128)(2,1)} %bitcast.16, bf16[8,32,3,24,256]{4,3,2,1,0:T(8,128)(2,1)} %bitcast.14), custom_call_target="tpu_custom_call" | custom-call | tf_op jit(solution)/shard_map/pallas_call | solution.py:271
  129.3 0.0 reduce-scatter.2.cloned.1.call-update
  129.3 11.1 %shard_map.122 = bf16[256,2688]{1,0:T(8,128)(2,1)} custom-call(bf16[320,768]{1,0:T(8,128)(2,1)} %get-tuple-element.23.gate_grad_ref, bf16[320,768]{1,0:T(8,128)(2,1)} %get-tuple-element.24.up_grad_ref, bf16[320,768]{1,0:T(8,128)(2,1)} %get-tuple-element.25.hidden_ref, bf16[8,320,256]{2,1,0:T(8,128)(2,1)} %get-tuple-element.26.scaled_ref, ...), custom_call_target="tpu_custom_call" | custom-call | tf_op jit(solution)/shard_map/pallas_call | solution.py:358
  140.4 8.9 %all-to-all-start.2 = ((bf16[32,8,2688]{2,1,0:T(8,128)(2,1)}), bf16[32,8,2688]{2,1,0:T(8,128)(2,1)S(1)}, u32[]{:S(2)}, u32[]{:S(2)}) async-start(bf16[32,8,2688]{2,1,0:T(8,128)(2,1)} %bitcast.17), calls=%async_computation.3 | async-start | bytes 2752512 | tf_op jit(solution)/shard_map/all_to_all | solution.py:456
  149.3 0.1 copy.14.slots_ref
  149.4 32.4 %all-to-all-done.2 = bf16[32,8,2688]{2,1,0:T(8,128)(2,1)S(1)} async-done(((bf16[32,8,2688]{2,1,0:T(8,128)(2,1)}), bf16[32,8,2688]{2,1,0:T(8,128)(2,1)S(1)}, u32[]{:S(2)}, u32[]{:S(2)}) %all-to-all-start.2) | async-done | bytes 1376288 | tf_op jit(solution)/shard_map/all_to_all | solution.py:456
  181.8 0.0 copy-start.3
  181.8 1.6 shard_map.123
  183.4 6.1 %reduce-scatter.2.cloned.1.call-done = bf16[1,32,3,24,256]{4,3,2,1,0:T(8,128)(2,1)} async-done(((bf16[8,32,3,24,256]{4,3,2,1,0:T(8,128)(2,1)}), bf16[1,32,3,24,256]{4,3,2,1,0:T(8,128)(2,1)}) %reduce-scatter.2.cloned.1.call-update) | async-done | bytes 1179664 | tf_op jit(solution)/shard_map/reduce_scatter | solution.py:474
  189.5 42.2 %all_to_all.21.part_ref = bf16[32,3,24,256]{3,2,1,0:T(8,128)(2,1)S(1)} all-to-all(bf16[32,3,24,256]{3,2,1,0:T(8,128)(2,1)} %bitcast.18), channel_id=1, replica_groups=mesh['dp'=8,'expert'=32] {'expert'}, dimensions={0} | all-to-all | bytes 2359296 | tf_op jit(solution)/shard_map/all_to_all | solution.py:456
  231.8 0.0 copy-done.3
  231.8 1.8 shard_map.124
  (1 shorter events, 0.0 us)
Async XLA Ops:
  9.9 11.4 %copy-start.4 = (bf16[128,2]{0,1:T(2,128)(2,1)S(1)}, bf16[128,2]{0,1:T(2,128)(2,1)}, u32[]{:S(2)}) copy-start(bf16[128,2]{0,1:T(2,128)(2,1)} %param.11) | copy-start | bytes 1540
  9.9 11.4 %copy-start = (bf16[128,2048]{1,0:T(8,128)(2,1)S(1)}, bf16[128,2048]{1,0:T(8,128)(2,1)}, u32[]{:S(2)}) copy-start(bf16[128,2048]{1,0:T(8,128)(2,1)} %tok_ref.1) | copy-start | bytes 1572868
  10.0 11.4 %copy-start.2 = (s32[128,2]{0,1:T(2,128)S(1)}, s32[128,2]{0,1:T(2,128)}, u32[]{:S(2)}) copy-start(s32[128,2]{0,1:T(2,128)} %param.10) | copy-start | bytes 3076
  10.0 38.8 %all-to-all-start = ((bf16[32,3,24,256]{3,2,1,0:T(8,128)(2,1)}), bf16[32,3,24,256]{3,2,1,0:T(8,128)(2,1)}, u32[]{:S(2)}, u32[]{:S(2)}) async-start(bf16[32,3,24,256]{3,2,1,0:T(8,128)(2,1)} %shard_map.119), calls=%async_computation | async-start | bytes 2359296 | tf_op jit(solution)/shard_map/all_to_all | solution.py:456
  21.3 94.3 %all-gather.3.cloned.1.call-start = ((), (), s32[]{:S(2)}) async-start(), calls=%async_computation.6 | async-start | bytes 10616832 | tf_op jit(solution)/shard_map/all_gather | solution.py:470
  21.4 1.0 copy-start.1
  48.8 140.7 %reduce-scatter.2.cloned.1.call-start = ((), (), s32[]{:S(2)}) async-start(), calls=%async_computation.5 | async-start | bytes 10616832 | tf_op jit(solution)/shard_map/reduce_scatter | solution.py:474
  140.4 41.4 %all-to-all-start.2 = ((bf16[32,8,2688]{2,1,0:T(8,128)(2,1)}), bf16[32,8,2688]{2,1,0:T(8,128)(2,1)S(1)}, u32[]{:S(2)}, u32[]{:S(2)}) async-start(bf16[32,8,2688]{2,1,0:T(8,128)(2,1)} %bitcast.17), calls=%async_computation.3 | async-start | bytes 2752512 | tf_op jit(solution)/shard_map/all_to_all | solution.py:456
  181.8 50.0 %copy-start.3 = (s32[32]{0:T(128)S(1)}, s32[32]{0:T(128)}, u32[]{:S(2)}) copy-start(s32[32]{0:T(128)} %placement_ref.3) | copy-start | bytes 388
Sparse Core Ops, SparseCore 0:
  48.9 57.1 all-gather.2
  129.4 60.0 reduce-scatter.1
